TPU v7x, 768 devices: a whole 4x8x12 slice. The times are simulated.
768 devices in a mesh: ia: 16 (over z_hi, y), ja: 6 (over z_lo), ka: 8 (over x, core).
Axes of the slice: x: 4, y: 8, z: 12 (z_hi: 2, z_lo: 6; z = z_hi * 6 + z_lo), core: 2. Of those that a mesh axis runs over, the one named last changes fastest.
Arguments:
- flow_state: float32 [128, 5, 96, 1024], P('ia', None, 'ja', 'ka'), may hold values from -1.5 to 7, as said below
- mode_shapes: float32 [64, 128, 96], P('ka', 'ia', 'ja'), may hold values from -1 to 1
- modal_coords: float32 [2, 64], replicated, may hold values from -0.5 to 0.5
- wall_mask: int32 [128, 96], P('ia', 'ja'), may hold values 0 or 1
Outputs:
- new_state: float32 [128, 5, 96, 1024], P('ia', None, 'ja', 'ka')
- gen_force: float32 [64], P('ka')
Inputs may be any that keep to these rules, and one draw needn't show every extreme that they name: `flow_state`: in every cell the density lies between 0.5 and 2 and the pressure 0.4 (energy - 0.5 |momentum|^2 / density) between 0.4 and 2.
All inputs are finite; a program needn't handle non-finite values. No bound on the sum of `wall_mask` on one device may be relied on, other than what follows from the above.
Results may differ from a plain program's by a relative error of at most 0.0003.
Values sent between devices are 32-bit elements; how exact they have to be, the bound alone decides.
A program may use at most 32 MiB of HBM per device.

v0:
```python
import math

import jax
import jax.numpy as jnp
from jax import lax
from jax.sharding import PartitionSpec as P

HEAT_RATIO = 1.4
SECTION_STEP = 0.2
STRAIN = 0.25
FAR_PRESSURE = 0.8
FAR_STATE = (1.0, 0.6, 0.0, 0.0, 0.8)


def spread(value, axis, source):
    kept = jnp.where(lax.axis_index(axis) == source, value, 0).astype(value.dtype)
    return lax.psum(kept, axis)


def with_halo(array, sides, width):
    for axis, dim in sides:
        size, length = (lax.axis_size(axis), array.shape[dim])
        up = [(i, (i + 1) % size) for i in range(size - 1)]
        down = [(j, i) for i, j in up]
        last = lax.slice_in_dim(array, length - width, length, axis=dim)
        initial = lax.slice_in_dim(array, 0, width, axis=dim)
        before = lax.ppermute(last, axis, up)
        after = lax.ppermute(initial, axis, down)
        array = jnp.concatenate([before, array, after], axis=dim)
    return array


def primitives(conserved):
    density = conserved[:, 0]
    along_x = conserved[:, 1] / density
    along_y = conserved[:, 2] / density
    along_z = conserved[:, 3] / density
    pressure = (HEAT_RATIO - 1.0) * (
        conserved[:, 4]
        - 0.5 * density * (along_x * along_x + along_y * along_y + along_z * along_z)
    )
    return jnp.stack([density, along_x, along_y, along_z, pressure], axis=1)


def minmod(first, second):
    return 0.5 * (jnp.sign(first) + jnp.sign(second)) * jnp.minimum(jnp.abs(first), jnp.abs(second))


def euler_flux(prim, component, grid_speed):
    density = prim[:, 0]
    along_x = prim[:, 1]
    along_y = prim[:, 2]
    along_z = prim[:, 3]
    pressure = prim[:, 4]
    normal_speed = prim[:, component] - grid_speed
    energy = pressure / (HEAT_RATIO - 1.0) + 0.5 * density * (
        along_x * along_x + along_y * along_y + along_z * along_z
    )
    conserved = [density, density * along_x, density * along_y, density * along_z, energy]
    fluxes = [quantity * normal_speed for quantity in conserved]
    fluxes[component] = fluxes[component] + pressure
    fluxes[4] = fluxes[4] + pressure * prim[:, component]
    wave = jnp.abs(normal_speed) + jnp.sqrt(HEAT_RATIO * pressure / density)
    return (jnp.stack(conserved, axis=1), jnp.stack(fluxes, axis=1), wave)


def face_fluxes(prim, direction, component, grid_speed):
    length = prim.shape[direction]
    cell_a = lax.slice_in_dim(prim, 0, length - 3, axis=direction)
    cell_b = lax.slice_in_dim(prim, 1, length - 2, axis=direction)
    cell_c = lax.slice_in_dim(prim, 2, length - 1, axis=direction)
    cell_d = lax.slice_in_dim(prim, 3, length, axis=direction)
    left_state = cell_b + 0.5 * minmod(cell_b - cell_a, cell_c - cell_b)
    right_state = cell_c - 0.5 * minmod(cell_c - cell_b, cell_d - cell_c)
    left_cons, left_flux, left_wave = euler_flux(left_state, component, grid_speed)
    right_cons, right_flux, right_wave = euler_flux(right_state, component, grid_speed)
    return 0.5 * (left_flux + right_flux) - 0.5 * jnp.maximum(left_wave, right_wave)[:, None] * (
        right_cons - left_cons
    )


def far_edges(padded, dim, own_index, final_index, far_b):
    extent = padded.shape[dim]
    shape_ones = [1, 1, 1, 1]
    shape_ones[dim] = extent
    positions = lax.broadcasted_iota(jnp.int32, tuple(shape_ones), dim)
    at_edge = (positions < 2) & (own_index == 0) | (positions >= extent - 2) & (
        own_index == final_index
    )
    return jnp.where(at_edge, far_b, padded)


def wall_edges(padded, wall_speed, wall_mask, far_b):
    extent = padded.shape[3]
    own_index = lax.axis_index("ka")
    final_index = lax.axis_size("ka") - 1
    positions = lax.broadcasted_iota(jnp.int32, (1, 1, 1, extent), 3)
    padded = jnp.where((positions >= extent - 2) & (own_index == final_index), far_b, padded)
    margin_i = (padded.shape[0] - wall_speed.shape[0]) // 2
    margin_j = (padded.shape[2] - wall_speed.shape[1]) // 2
    speed_padded = jnp.pad(wall_speed, ((margin_i, margin_i), (margin_j, margin_j)))
    mask_padded = jnp.pad(wall_mask, ((margin_i, margin_i), (margin_j, margin_j)))
    mirror = padded[..., 2:4][..., ::-1]
    reflected = 2.0 * speed_padded[:, :, None] - mirror[:, 3]
    mirror = jnp.concatenate([mirror[:, 0:3], reflected[:, None], mirror[:, 4:5]], axis=1)
    lower_rim = jnp.where(mask_padded[:, None, :, None] == 1, mirror, far_b)
    lower_rim = jnp.where(own_index == 0, lower_rim, padded[..., 0:2])
    return jnp.concatenate([lower_rim, padded[..., 2:]], axis=3)


def local(flow_state, mode_shapes, modal_coords, wall_mask):
    highest = lax.Precision.HIGHEST
    rows_i, rows_k = (flow_state.shape[0], flow_state.shape[3])
    total_i = rows_i * lax.axis_size("ia")
    total_j = flow_state.shape[2] * lax.axis_size("ja")
    total_k = rows_k * lax.axis_size("ka")
    index_i = lax.axis_index("ia")
    final_i = lax.axis_size("ia") - 1
    index_j = lax.axis_index("ja")
    final_j = lax.axis_size("ja") - 1
    far_b = jnp.array(FAR_STATE, jnp.float32).reshape(1, 5, 1, 1)
    modes_here = mode_shapes.shape[0]
    first_mode = lax.axis_index("ka") * modes_here
    own_coords = lax.dynamic_slice_in_dim(modal_coords, first_mode, modes_here, 1)
    partial_planes = jnp.einsum("cm,mij->cij", own_coords, mode_shapes, precision=highest)
    surface_planes = lax.psum(partial_planes, "ka")
    displacement = surface_planes[0]
    wall_speed = surface_planes[1]
    prim = primitives(flow_state)
    wall_load = jnp.where(wall_mask == 1, prim[:, 4, :, 0] - FAR_PRESSURE, 0.0)
    wall_plane = spread(wall_load, "ka", 0)
    forces_local = jnp.einsum("mij,ij->m", mode_shapes, wall_plane, precision=highest)
    gen_force = lax.psum(forces_local, ("ia", "ja")) / math.sqrt(total_i * total_j)
    first_cell = lax.axis_index("ka") * rows_k
    face_pos = (first_cell + jnp.arange(rows_k + 1, dtype=jnp.int32)).astype(jnp.float32) / total_k
    cell_pos = (
        (first_cell + jnp.arange(rows_k, dtype=jnp.int32)).astype(jnp.float32) + 0.5
    ) / total_k
    grid_speed = ((1.0 - face_pos) ** 2)[None, None, :] * wall_speed[:, :, None]
    padded = with_halo(prim, (("ia", 0), ("ja", 2), ("ka", 3)), 2)
    padded = far_edges(padded, 0, index_i, final_i, far_b)
    padded = far_edges(padded, 2, index_j, final_j, far_b)
    padded = wall_edges(padded, wall_speed, wall_mask, far_b)
    flux_i = face_fluxes(padded[:, :, 2:-2, 2:-2], 0, 1, 0.0)
    flux_j = face_fluxes(padded[2:-2, :, :, 2:-2], 2, 2, 0.0)
    flux_k = face_fluxes(padded[2:-2, :, 2:-2, :], 3, 3, grid_speed)
    residual = (
        flux_i[1:]
        - flux_i[:-1]
        + (flux_j[:, :, 1:] - flux_j[:, :, :-1])
        + (flux_k[..., 1:] - flux_k[..., :-1])
    )
    volume_ratio = jnp.exp(-STRAIN * (1.0 - cell_pos)[None, None, :] * displacement[:, :, None])
    new_state = flow_state - SECTION_STEP * residual / volume_ratio[:, None]
    return (new_state, gen_force)


def solution(mesh):
    placed = (P("ia", None, "ja", "ka"), P("ka", "ia", "ja"), P(), P("ia", "ja"))
    return jax.shard_map(
        local,
        mesh=mesh,
        in_specs=placed,
        out_specs=(P("ia", None, "ja", "ka"), P("ka")),
        check_vma=False,
    )
```

profile of v0, /device:TPU:33, one launch (start us, length us, event | category | flops | bytes accessed | tf_op | source)
XLA Modules:
  0.0 384.9 jit_solution(617801561190887324)
XLA Ops:
  0.7 0.9 constant_dynamic-update-slice_fusion.4
  1.5 0.9 constant_dynamic-update-slice_fusion.3
  2.4 0.9 constant_dynamic-update-slice_fusion.2
  3.3 0.9 constant_dynamic-update-slice_fusion.1
  4.2 1.0 constant_dynamic-update-slice_fusion
  5.3 2.3 collective-permute-start
  7.6 4.2 %collective-permute-start.1 = (f32[2,5,16,128]{3,2,1,0:T(8,128)S(1)}, f32[2,5,16,128]{3,2,1,0:T(8,128)S(1)}, u32[]{:S(2)}, u32[]{:S(2)}) collective-permute-start(f32[2,5,16,128]{3,2,1,0:T(8,128)S(1)} %get-tuple-element.50), channel_id=1, source_target_pairs={{48,0},{96,48},{144,96},{192,144},{240,192},{288,240},{336,288},{3... | collective-permute-start | bytes 245768 | tf_op jit(solution)/shard_map/ppermute | solution.py:28
  12.9 22.8 %all-reduce.2 = (f32[2,8,16]{2,0,1:T(2,128)S(1)}, f32[8,16]{1,0:T(8,128)S(1)}) all-reduce(f32[2,8,16]{2,0,1:T(2,128)S(1)} %fusion.11, f32[8,16]{1,0:T(8,128)S(1)} %select_select_fusion), channel_id=1, replica_groups=mesh['ia'=16,'ja'=6,'ka'=8] {'ka'}, use_global_device_ids=true, to_apply=%region_0.0 | all-reduce | flops 384 | bytes 3072 | tf_op jit(solution)/shard_map/psum | solution.py:126
  36.4 262.3 %psum.23 = f32[8]{0:T(128)S(1)} all-reduce(f32[8]{0:T(128)S(1)} %convolution_bitcast_fusion), channel_id=1, replica_groups=mesh['ia'=16,'ja'=6,'ka'=8] {'ia','ja'}, use_global_device_ids=true, to_apply=%region_2.3 | all-reduce | flops 8 | bytes 64 | tf_op jit(solution)/shard_map/psum | solution.py:133
  299.2 0.7 multiply_exponential_fusion
  300.0 1.3 collective-permute-start.2
  301.3 1.3 collective-permute-start.3
  302.7 3.9 %collective-permute-done.3 = f32[12,5,2,128]{3,2,1,0:T(2,128)S(1)} collective-permute-done((f32[12,5,2,128]{3,2,1,0:T(2,128)S(1)}, f32[12,5,2,128]{3,2,1,0:T(2,128)S(1)}, u32[]{:S(2)}, u32[]{:S(2)}) %collective-permute-start.3) | collective-permute-done | bytes 61472 | tf_op jit(solution)/shard_map/ppermute | solution.py:28
  308.1 46.5 %collective-permute-start.4 = (f32[12,5,20,2]{2,3,1,0:T(2,128)S(1)}, f32[12,5,20,2]{2,3,1,0:T(2,128)S(1)}, u32[]{:S(2)}, u32[]{:S(2)}) collective-permute-start(f32[12,5,20,2]{2,3,1,0:T(2,128)S(1)} %copy.119), channel_id=1, source_target_pairs={{0,1},{1,2},{2,3},{3,4},{4,5},{5,6},{6,7},{8,9},{9,10},{10,11},{11... | collective-permute-start | bytes 28808 | tf_op jit(solution)/shard_map/ppermute | solution.py:27
  355.1 3.1 collective-permute-start.5
  359.3 1.3 collective-permute-done.5
  361.1 1.7 fusion.1
  363.4 0.9 multiply_add_fusion.1
  364.3 0.9 fusion.16
  366.0 0.7 multiply_bitcast_fusion.2
  366.7 0.7 constant_dynamic-update-slice_fusion.5
  369.0 0.8 multiply_bitcast_fusion.1
  369.9 0.8 constant_dynamic-update-slice_fusion.25
  370.7 0.7 copy-done.6
  371.8 0.8 copy-done.4
  372.6 1.7 slice.294
  374.2 1.0 slice.291
  375.2 1.0 slice.296
  376.2 1.0 broadcast_subtract_fusion
  377.3 1.2 slice_select_fusion
  378.5 1.2 multiply_add_fusion
  384.0 0.9 fusion.7
  (130 shorter events, 13.4 us)
Async XLA Ops:
  0.6 12.0 %copy-start = (f32[8,8,16]{2,1,0:T(8,128)S(1)}, f32[8,8,16]{2,1,0:T(8,128)}, u32[]{:S(2)}) copy-start(f32[8,8,16]{2,1,0:T(8,128)} %param.6) | copy-start | bytes 12292
  0.6 11.3 %copy-start.26 = (s32[8,16]{1,0:T(8,128)S(1)}, s32[8,16]{1,0:T(8,128)}, u32[]{:S(2)}) copy-start(s32[8,16]{1,0:T(8,128)} %param.8) | copy-start | bytes 1540
  0.7 12.0 %copy-start.30 = (f32[2,64]{1,0:T(2,128)S(1)}, f32[2,64]{1,0:T(2,128)}, u32[]{:S(2)}) copy-start(f32[2,64]{1,0:T(2,128)} %param.7) | copy-start | bytes 1540
  5.3 294.7 %collective-permute-start = (f32[2,5,16,128]{3,2,1,0:T(8,128)S(1)}, f32[2,5,16,128]{3,2,1,0:T(8,128)S(1)}, u32[]{:S(2)}, u32[]{:S(2)}) collective-permute-start(f32[2,5,16,128]{3,2,1,0:T(8,128)S(1)} %get-tuple-element.49), channel_id=1, source_target_pairs={{0,48},{48,96},{96,144},{144,192},{192,240},{240,288},{288,336},{3... | collective-permute-start | bytes 245768 | tf_op jit(solution)/shard_map/ppermute | solution.py:27
  7.6 292.4 %collective-permute-start.1 = (f32[2,5,16,128]{3,2,1,0:T(8,128)S(1)}, f32[2,5,16,128]{3,2,1,0:T(8,128)S(1)}, u32[]{:S(2)}, u32[]{:S(2)}) collective-permute-start(f32[2,5,16,128]{3,2,1,0:T(8,128)S(1)} %get-tuple-element.50), channel_id=1, source_target_pairs={{48,0},{96,48},{144,96},{192,144},{240,192},{288,240},{336,288},{3... | collective-permute-start | bytes 245768 | tf_op jit(solution)/shard_map/ppermute | solution.py:28
  300.0 2.6 collective-permute-start.2
  301.3 5.3 %collective-permute-start.3 = (f32[12,5,2,128]{3,2,1,0:T(2,128)S(1)}, f32[12,5,2,128]{3,2,1,0:T(2,128)S(1)}, u32[]{:S(2)}, u32[]{:S(2)}) collective-permute-start(f32[12,5,2,128]{3,2,1,0:T(2,128)S(1)} %get-tuple-element.41), channel_id=1, source_target_pairs={{8,0},{16,8},{24,16},{32,24},{40,32},{9,1},{17,9},{25,17},{33,25},... | collective-permute-start | bytes 184328 | tf_op jit(solution)/shard_map/ppermute | solution.py:28
  307.6 53.5 %copy-start.28 = (f32[5]{0:T(128)S(1)}, f32[5]{0:T(128)}, u32[]{:S(2)}) copy-start(f32[5]{0:T(128)} %constant.26.clone) | copy-start | bytes 64
  308.1 50.7 %collective-permute-start.4 = (f32[12,5,20,2]{2,3,1,0:T(2,128)S(1)}, f32[12,5,20,2]{2,3,1,0:T(2,128)S(1)}, u32[]{:S(2)}, u32[]{:S(2)}) collective-permute-start(f32[12,5,20,2]{2,3,1,0:T(2,128)S(1)} %copy.119), channel_id=1, source_target_pairs={{0,1},{1,2},{2,3},{3,4},{4,5},{5,6},{6,7},{8,9},{9,10},{10,11},{11... | collective-permute-start | bytes 28808 | tf_op jit(solution)/shard_map/ppermute | solution.py:27
  355.1 5.5 %collective-permute-start.5 = (f32[12,5,20,2]{2,3,1,0:T(2,128)S(1)}, f32[12,5,20,2]{2,3,1,0:T(2,128)S(1)}, u32[]{:S(2)}, u32[]{:S(2)}) collective-permute-start(f32[12,5,20,2]{2,3,1,0:T(2,128)S(1)} %copy.120), channel_id=1, source_target_pairs={{1,0},{2,1},{3,2},{4,3},{5,4},{6,5},{7,6},{9,8},{10,9},{11,10},{12... | collective-permute-start | bytes 28808 | tf_op jit(solution)/shard_map/ppermute | solution.py:28
  367.4 0.9 copy-start.12
  367.4 1.0 copy-start.14
  369.8 6.4 %copy-start.25 = (f32[12,20]{1,0:T(8,128)S(1)}, f32[12,20]{1,0:T(8,128)}, u32[]{:S(2)}) copy-start(f32[12,20]{1,0:T(8,128)} %pad_multiply_fusion) | copy-start | bytes 2884
  370.6 1.0 copy-start.8
  370.6 6.6 %copy-start.27 = (pred[12,20]{1,0:T(8,128)(4,1)S(1)}, pred[12,20]{1,0:T(8,128)(4,1)}, u32[]{:S(2)}) copy-start(pred[12,20]{1,0:T(8,128)(4,1)} %pad_compare_fusion) | copy-start | bytes 724
  370.6 6.6 %copy-start.29 = (f32[5]{0:T(128)S(1)}, f32[5]{0:T(128)}, u32[]{:S(2)}) copy-start(f32[5]{0:T(128)} %constant.26.clone) | copy-start | bytes 64
  370.7 1.1 copy-start.2
  380.4 1.0 copy-start.15
  380.4 1.0 copy-start.21
  380.5 1.1 copy-start.17
  380.5 1.2 copy-start.3
  380.6 1.2 copy-start.20
  380.6 1.4 copy-start.5
  380.6 1.4 copy-start.19
  380.7 1.4 copy-start.11
  380.7 1.5 copy-start.13
  380.7 1.5 copy-start.22
  381.6 1.2 copy-start.7
  381.6 1.3 copy-start.9
  381.6 1.3 copy-start.18
  383.1 1.0 copy-start.1
  383.1 1.0 copy-start.23
  (5 other events, 3.7 us)
where the time goes:
time: 386 us; the launch traced here: 385 us
  blocking collectives  285 us (74%)
  starting transfers between devices  58.7 us (15%)
  other arithmetic  19.5 us (5%)
  local copies, waits for them, and re-layouts  14.7 us (4%)
  waiting for transfers between devices  5.27 us (1%)
    psum x1, blocking collectives, local(): lax.psum(forces_local, ('ia', 'ja')) / math.sqrt(total_i * total_j)  262 us
    ppermute x3, starting transfers between devices, with_halo(): before = lax.ppermute(last, axis, up)  50.1 us
    psum x1, blocking collectives, local(): surface_planes = lax.psum(partial_planes, 'ka')  22.8 us
    ppermute x3, starting transfers between devices, with_halo(): after = lax.ppermute(initial, axis, down)  8.6 us
    unnamed x65, local copies, waits for them, and re-layouts  8.31 us
  transfers between devices with their start and end apart: 6, of which 2 were waited for; matrix products, arithmetic and copies ran while one was open for 1% of the time, Pallas kernels for 0%

commit v1 on v0

v1 whole, which is shorter than its diff:
```python
import functools
import math

import jax
import jax.numpy as jnp
from jax import lax
from jax.experimental import pallas as pl
from jax.experimental.pallas import tpu as pltpu
from jax.sharding import PartitionSpec as P

MESH = pl.DeviceIdType.MESH
SECTION_STEP = 0.2
STRAIN = 0.25
FAR_PRESSURE = 0.8
FAR_STATE = (1.0, 0.6, 0.0, 0.0, 0.8)


def primitives(block):
    density, mom_x, mom_y, mom_z, energy = block
    inverse = 1.0 / density
    pressure = 0.4 * (energy - 0.5 * (mom_x * mom_x + mom_y * mom_y + mom_z * mom_z) * inverse)
    return [density, mom_x * inverse, mom_y * inverse, mom_z * inverse, pressure]


def minmod(x, y):
    return jnp.maximum(jnp.minimum(x, jnp.maximum(y, 0.0)), jnp.minimum(y, 0.0))


def side_flux(state, component, grid_speed):
    density, along_x, along_y, along_z, pressure = state
    own = state[component]
    normal = own if grid_speed is None else own - grid_speed
    mom = [density * along_x, density * along_y, density * along_z]
    energy = 2.5 * pressure + 0.5 * (mom[0] * along_x + mom[1] * along_y + mom[2] * along_z)
    conserved = [density] + mom + [energy]
    flux = [quantity * normal for quantity in conserved]
    flux[component] = flux[component] + pressure
    flux[4] = flux[4] + pressure * own
    wave = jnp.abs(normal) + math.sqrt(1.4) * pressure * lax.rsqrt(pressure * density)
    return conserved, flux, wave


def faces(a, b, c, d, component, grid_speed=None):
    left, right = [], []
    for wa, wb, wc, wd in zip(a, b, c, d):
        middle = wc - wb
        left.append(wb + 0.5 * minmod(wb - wa, middle))
        right.append(wc - 0.5 * minmod(middle, wd - wc))
    left_cons, left_flux, left_wave = side_flux(left, component, grid_speed)
    right_cons, right_flux, right_wave = side_flux(right, component, grid_speed)
    wave = jnp.maximum(left_wave, right_wave)
    return [
        lf + rf - wave * (rc - lc)
        for lf, rf, lc, rc in zip(left_flux, right_flux, left_cons, right_cons)
    ]


def section(
    sizes, flow, shapes, coords, mask, new, force,
    fv, sv, mv, prim, raw_i, raw_j, send_k, halo_k, edge_k, planes, planes_in,
    s_own, l_own, s_all, l_all, g_own, g_in, flux_i,
    local_sem, send_sem, recv_sem, many_sem,
):
    ni, nj, nk = sizes
    ia, ja, ka = lax.axis_index("ia"), lax.axis_index("ja"), lax.axis_index("ka")
    li, lj, lk = flow.shape[0], flow.shape[2], flow.shape[3]
    modes = shapes.shape[0]
    columns = ni * nj
    column = ia * nj + ja
    is_root = column == 0
    total_k = nk * lk

    in_flow = pltpu.make_async_copy(flow, fv, local_sem.at[0])
    in_shapes = pltpu.make_async_copy(shapes, sv, local_sem.at[1])
    in_mask = pltpu.make_async_copy(mask, mv, local_sem.at[2])
    in_flow.start()
    in_shapes.start()
    in_mask.start()

    barrier = pltpu.get_barrier_semaphore()

    def greet(where):
        pl.semaphore_signal(barrier, inc=1, device_id=where, device_id_type=MESH)

    @pl.when(is_root)
    def _():
        @pl.loop(1, columns)
        def _(c):
            greet({"ia": c // nj, "ja": lax.rem(c, nj)})

        @pl.when(ka > 0)
        def _():
            @pl.loop(0, columns)
            def _(c):
                greet({"ia": c // nj, "ja": lax.rem(c, nj), "ka": 0})

    beside = [
        (ia > 0, {"ia": jnp.maximum(ia - 1, 0)}),
        (ia < ni - 1, {"ia": jnp.minimum(ia + 1, ni - 1)}),
        (ja > 0, {"ja": jnp.maximum(ja - 1, 0)}),
        (ja < nj - 1, {"ja": jnp.minimum(ja + 1, nj - 1)}),
    ]
    expected = nk - 1
    for there, where in beside:
        pl.when(there)(functools.partial(greet, where))
        expected = expected + there.astype(jnp.int32)
    for o in range(1, nk):
        greet({"ka": lax.rem(ka + o, nk)})
    expected = expected + jnp.where(is_root, 0, 1) + jnp.where(ka == 0, nk - 1, 0)

    lane = lax.broadcasted_iota(jnp.int32, (8, 128), 1)

    in_shapes.wait()
    in_mask.wait()
    packed = jnp.zeros((li, 128), jnp.float32)
    disp = jnp.zeros((li, lj), jnp.float32)
    speed = jnp.zeros((li, lj), jnp.float32)
    zeros = jnp.zeros((li, 128 - lj), jnp.float32)
    for m in range(modes):
        one = sv[m]
        wide = jnp.concatenate([one, zeros], axis=1)
        packed = packed + (pltpu.roll(wide, lj * m, 1) if m else wide)
        disp = disp + coords[0, ka * modes + m] * one
        speed = speed + coords[1, ka * modes + m] * one
    s_own[...] = packed
    planes[...] = jnp.concatenate([disp, speed, jnp.zeros((li, 128 - 2 * lj), jnp.float32)], axis=1)

    in_flow.wait()

    @pl.when(ka == 0)
    def _():
        lane_t = lax.broadcasted_iota(jnp.int32, (lj, 128), 1)
        turned = jnp.zeros((lj, 128), jnp.float32)
        for i in range(li):
            p = primitives([fv[i, c, :, 0:1] for c in range(5)])[4]
            turned = turned + jnp.where(lax.rem(lane_t, li) == i, p - FAR_PRESSURE, 0.0)
        flat = jnp.concatenate([turned] * (128 // lj), axis=0).T[0:li]
        keep = jnp.concatenate([mv[...]] * (128 // lj), axis=1)
        l_own[...] = jnp.where(keep == 1, flat, 0.0)

    pl.semaphore_wait(barrier, expected)

    def to_root(src, dst, sem_index, recv, where):
        return pltpu.make_async_remote_copy(
            src_ref=src, dst_ref=dst, send_sem=send_sem.at[sem_index], recv_sem=recv,
            device_id=where, device_id_type=MESH,
        )

    root_here = {"ia": 0, "ja": 0}
    load_copies = [
        to_root(l_own, l_all.at[column], 8 + o, many_sem.at[1], {"ia": 0, "ja": 0, "ka": o})
        for o in range(nk)
    ]
    shape_copy = to_root(s_own, s_all.at[column], 7, many_sem.at[0], root_here)

    @pl.when(ka == 0)
    def _():
        for o, copy in enumerate(load_copies):
            if o:
                copy.start()
            else:
                pl.when(~is_root)(copy.start)

    pl.when(~is_root)(shape_copy.start)

    @pl.when(is_root)
    def _():
        s_all[0] = s_own[...]

        @pl.when(ka == 0)
        def _():
            l_all[0] = l_own[...]

    def halo(src, dst, index, where):
        return pltpu.make_async_remote_copy(
            src_ref=src, dst_ref=dst, send_sem=send_sem.at[index], recv_sem=recv_sem.at[index],
            device_id=where, device_id_type=MESH,
        )

    (has_i0, to_i0), (has_i1, to_i1), (has_j0, to_j0), (has_j1, to_j1) = beside
    has_k0, has_k1 = ka > 0, ka < nk - 1
    copies = [
        (halo(flow.at[li - 2 : li], raw_i.at[0], 0, to_i1), has_i1, has_i0),
        (halo(flow.at[0:2], raw_i.at[1], 1, to_i0), has_i0, has_i1),
        (halo(flow.at[:, :, lj - 8 : lj], raw_j.at[0], 2, to_j1), has_j1, has_j0),
        (halo(flow.at[:, :, 0:8], raw_j.at[1], 3, to_j0), has_j0, has_j1),
        (halo(send_k.at[0], halo_k.at[0], 4, {"ka": jnp.minimum(ka + 1, nk - 1)}), has_k1, has_k0),
        (halo(send_k.at[1], halo_k.at[1], 5, {"ka": jnp.maximum(ka - 1, 0)}), has_k0, has_k1),
    ]
    for copy, sends, _ in copies[0:4]:
        pl.when(sends)(copy.start)

    plane_copies = [
        pltpu.make_async_remote_copy(
            src_ref=planes, dst_ref=planes_in.at[o - 1], send_sem=send_sem.at[15 + o],
            recv_sem=many_sem.at[2], device_id={"ka": lax.rem(ka + o, nk)}, device_id_type=MESH,
        )
        for o in range(1, nk)
    ]
    for copy in plane_copies:
        copy.start()

    lane_j = lax.broadcasted_iota(jnp.int32, (lj, 128), 1)
    send_k[...] = jnp.zeros_like(send_k)

    @pl.loop(0, li)
    def _(i):
        here = lane_j // 2 == i
        for c, w in enumerate(primitives([fv[i, c] for c in range(5)])):
            prim[i + 2, c, 8 : 8 + lj] = w
            send_k[0, c] = jnp.where(here, pltpu.roll(w, 2 * i + 2, 1), send_k[0, c])
            send_k[1, c] = jnp.where(here, pltpu.roll(w, 2 * i, 1), send_k[1, c])

    for copy, sends, _ in copies[4:6]:
        pl.when(sends)(copy.start)

    def far(shape, c):
        return jnp.full(shape, FAR_STATE[c], jnp.float32)

    pltpu.make_async_copy(planes_in, planes_in, many_sem.at[2]).wait()
    total = planes[...]
    for o in range(nk - 1):
        total = total + planes_in[o]
    wall = mv[...].astype(jnp.float32)
    wall = jnp.concatenate([jnp.zeros((li, 2 * lj), jnp.float32), wall, jnp.zeros((li, 128 - 3 * lj), jnp.float32)], axis=1)
    turned = jnp.concatenate([total + wall, jnp.zeros((128 - li, 128), jnp.float32)], axis=0).T

    for side, (base, (copy, _, gets)) in enumerate(zip((0, li + 2), copies[0:2])):

        @pl.when(gets)
        def _(side=side, base=base, copy=copy):
            copy.wait_recv()
            for r in range(2):
                for c, w in enumerate(primitives([raw_i[side, r, c] for c in range(5)])):
                    prim[base + r, c, 8 : 8 + lj] = w

        @pl.when(~gets)
        def _(base=base):
            for r in range(2):
                for c in range(5):
                    prim[base + r, c, 8 : 8 + lj] = far((lj, lk), c)

    for side, (base, (copy, _, gets)) in enumerate(zip((0, 8 + lj), copies[2:4])):

        @pl.when(gets)
        def _(side=side, base=base, copy=copy):
            copy.wait_recv()

            @pl.loop(0, li)
            def _(i):
                for c, w in enumerate(primitives([raw_j[side, i, c] for c in range(5)])):
                    prim[i + 2, c, base : base + 8] = w

        @pl.when(~gets)
        def _(base=base):
            @pl.loop(0, li)
            def _(i):
                for c in range(5):
                    prim[i + 2, c, base : base + 8] = far((8, lk), c)

    pl.when(has_k0)(copies[4][0].wait_recv)
    pl.when(has_k1)(copies[5][0].wait_recv)

    @pl.when(~has_k0)
    def _():
        halo_k[0] = jnp.zeros(halo_k.shape[1:], jnp.float32)

    @pl.when(~has_k1)
    def _():
        for c in range(5):
            halo_k[1, c] = far((lj, 128), c)

    first = ka * lk
    own_pair = [send_k[0, c] for c in range(5)]
    next_pair = [halo_k[1, c] for c in range(5)]
    last_weight = (1.0 - (first + lk).astype(jnp.float32) / total_k) ** 2
    speed_pairs = jnp.zeros((lj, 128), jnp.float32)
    for i in range(li):
        speed_pairs = jnp.where(lane_j // 2 == i, turned[lj : 2 * lj, i : i + 1], speed_pairs)
    last = faces(
        own_pair,
        [pltpu.roll(w, 127, 1) for w in own_pair],
        next_pair,
        [pltpu.roll(w, 127, 1) for w in next_pair],
        3,
        last_weight * speed_pairs,
    )
    for c in range(5):
        edge_k[c] = last[c]

    def cells(i, lo, rows):
        return [prim[i, c, lo : lo + rows] for c in range(5)]

    def along_i(i):
        return faces(cells(i, 8, lj), cells(i + 1, 8, lj), cells(i + 2, 8, lj), cells(i + 3, 8, lj), 1)

    for c, w in enumerate(along_i(0)):
        flux_i[c] = w
    at_wall = ka == 0
    lane_f = (first + lane_j).astype(jnp.float32)
    face_weight = (1.0 - lane_f / total_k) ** 2
    cell_weight = STRAIN * (1.0 - (lane_f + 0.5) / total_k)
    first_lane, pair_lane, last_lane = lane_j < 1, lane_j < 2, lane_j == lk - 1
    column_lane = lax.broadcasted_iota(jnp.int32, (3 * lj, 128), 1)

    @pl.loop(0, li)
    def _(i):
        column_i = jnp.sum(jnp.where(column_lane == i, turned[0 : 3 * lj], 0.0), axis=1, keepdims=True)
        disp_i = column_i[0:lj]
        speed_i = jnp.broadcast_to(column_i[lj : 2 * lj], (lj, 128))
        solid = jnp.broadcast_to(column_i[2 * lj : 3 * lj], (lj, 128)) > 0.5

        upper = along_i(i + 1)
        residual = []
        for c in range(5):
            residual.append(upper[c] - flux_i[c])
            flux_i[c] = upper[c]

        rows = lj + 8
        flux_j = faces(cells(i + 2, 6, rows), cells(i + 2, 7, rows), cells(i + 2, 8, rows), cells(i + 2, 9, rows), 2)
        residual = [r + (f[1 : lj + 1] - f[0:lj]) for r, f in zip(residual, flux_j)]

        below2, below, above = [], [], []
        own = cells(i + 2, 8, lj)
        for c, w in enumerate(own):
            up = jnp.where(last_lane, pltpu.roll(halo_k[1, c], lk - 1 - 2 * i, 1), pltpu.roll(w, lk - 1, 1))
            down = pltpu.roll(w, 1, 1)
            mirror2 = jnp.where(first_lane, up, down)
            mirror1 = w
            if c == 3:
                mirror2 = 2.0 * speed_i - mirror2
                mirror1 = 2.0 * speed_i - mirror1
            mirror2 = jnp.where(solid, mirror2, FAR_STATE[c])
            mirror1 = jnp.where(solid, mirror1, FAR_STATE[c])
            ghost = halo_k[0, c]
            ghost2 = jnp.where(at_wall, mirror2, pltpu.roll(ghost, lax.rem(lk - 2 * i, lk), 1))
            ghost1 = jnp.where(at_wall, mirror1, pltpu.roll(ghost, lk - 1 - 2 * i, 1))
            below2.append(jnp.where(pair_lane, ghost2, pltpu.roll(w, 2, 1)))
            below.append(jnp.where(first_lane, ghost1, down))
            above.append(up)
        flux_k = faces(below2, below, own, above, 3, face_weight * speed_i)
        growth = (-0.5 * SECTION_STEP) * jnp.exp(cell_weight * disp_i)
        for c, f in enumerate(flux_k):
            end = pltpu.roll(edge_k[c], lk - 1 - 2 * i, 1)
            high = jnp.where(last_lane, end, pltpu.roll(f, lk - 1, 1))
            new[i, c] = fv[i, c] + growth * (residual[c] + (high - f))

    @pl.when(is_root)
    def _():
        others = s_all.at[1:columns]
        pltpu.make_async_copy(others, others, many_sem.at[0]).wait()

        @pl.when(ka == 0)
        def _():
            loads = l_all.at[1:columns]
            pltpu.make_async_copy(loads, loads, many_sem.at[1]).wait()

        @pl.when(ka > 0)
        def _():
            pltpu.make_async_copy(l_all, l_all, many_sem.at[1]).wait()

        g_own[...] = jnp.sum(s_all[...] * l_all[...], axis=0)

        @pl.loop(1, columns)
        def _(c):
            pltpu.make_async_remote_copy(
                src_ref=g_own, dst_ref=g_in, send_sem=many_sem.at[4], recv_sem=many_sem.at[3],
                device_id={"ia": c // nj, "ja": lax.rem(c, nj)}, device_id_type=MESH,
            ).start()

        force[...] = g_own[...]

    @pl.when(~is_root)
    def _():
        pltpu.make_async_copy(g_in, g_in, many_sem.at[3]).wait()
        force[...] = g_in[...]

    for copy, sends, _ in copies:
        pl.when(sends)(copy.wait_send)
    for copy in plane_copies:
        copy.wait_send()
    pl.when(~is_root)(shape_copy.wait_send)

    @pl.when(ka == 0)
    def _():
        for o, copy in enumerate(load_copies):
            if o:
                copy.wait_send()
            else:
                pl.when(~is_root)(copy.wait_send)

    @pl.when(is_root)
    def _():
        others = s_all.at[1:columns]
        pltpu.make_async_copy(others, others, many_sem.at[4]).wait()


def finish(scale, new, partial, out, force, sem):
    copy = pltpu.make_async_copy(new, out, sem)
    copy.start()
    group = partial.shape[1] // 8
    row = lax.broadcasted_iota(jnp.int32, (8, 128), 0)
    lane = lax.broadcasted_iota(jnp.int32, (8, 128), 1)
    summed = jnp.sum(partial[...], axis=0, keepdims=True)
    each = jnp.sum(jnp.where(lane // group == row, summed, 0.0), axis=1, keepdims=True)
    force[...] = jnp.sum(jnp.where(lane == row, each, 0.0), axis=0, keepdims=True)[:, 0:8] * scale
    copy.wait()


def solution(mesh):
    sizes = (mesh.shape["ia"], mesh.shape["ja"], mesh.shape["ka"])
    ni, nj, nk = sizes

    def local(flow_state, mode_shapes, modal_coords, wall_mask):
        li, _, lj, lk = flow_state.shape
        modes = mode_shapes.shape[0]
        f32 = jnp.float32
        tile = pltpu.VMEM((8, 128), f32)
        vmem = pl.BlockSpec(memory_space=pltpu.VMEM)
        hbm = pl.BlockSpec(memory_space=pltpu.HBM)
        free = pl.BlockSpec(memory_space=pl.ANY)
        new, partial = pl.pallas_call(
            functools.partial(section, sizes),
            out_shape=(
                jax.ShapeDtypeStruct(flow_state.shape, f32),
                jax.ShapeDtypeStruct((8, 128), f32),
            ),
            in_specs=[hbm, hbm, pl.BlockSpec(memory_space=pltpu.SMEM), hbm],
            out_specs=(vmem, vmem),
            scratch_shapes=[
                pltpu.VMEM(flow_state.shape, f32),
                pltpu.VMEM(mode_shapes.shape, f32),
                pltpu.VMEM(wall_mask.shape, jnp.int32),
                pltpu.VMEM((li + 4, 5, lj + 24, lk), f32),
                pltpu.VMEM((2, 2, 5, lj, lk), f32),
                pltpu.VMEM((2, li, 5, 8, lk), f32),
                pltpu.VMEM((2, 5, lj, 128), f32),
                pltpu.VMEM((2, 5, lj, 128), f32),
                pltpu.VMEM((5, lj, 128), f32),
                tile,
                pltpu.VMEM((nk - 1, 8, 128), f32),
                tile,
                tile,
                pltpu.VMEM((ni * nj, 8, 128), f32),
                pltpu.VMEM((ni * nj, 8, 128), f32),
                tile,
                tile,
                pltpu.VMEM((5, lj, lk), f32),
                pltpu.SemaphoreType.DMA((3,)),
                pltpu.SemaphoreType.DMA((15 + nk,)),
                pltpu.SemaphoreType.DMA((6,)),
                pltpu.SemaphoreType.DMA((5,)),
            ],
            compiler_params=pltpu.CompilerParams(
                collective_id=0, has_side_effects=True, vmem_limit_bytes=32 * 1024 * 1024
            ),
            name="section",
        )(flow_state, mode_shapes, modal_coords, wall_mask)
        out, force = pl.pallas_call(
            functools.partial(finish, 1.0 / math.sqrt(ni * li * nj * lj)),
            out_shape=(
                jax.ShapeDtypeStruct(flow_state.shape, f32),
                jax.ShapeDtypeStruct((1, modes), f32),
            ),
            in_specs=[free, vmem],
            out_specs=(hbm, vmem),
            scratch_shapes=[pltpu.SemaphoreType.DMA],
            name="finish",
        )(new, partial)
        return (out, force.reshape(modes))

    return jax.shard_map(
        local,
        mesh=mesh,
        in_specs=(P("ia", None, "ja", "ka"), P("ka", "ia", "ja"), P(), P("ia", "ja")),
        out_specs=(P("ia", None, "ja", "ka"), P("ka")),
        check_vma=False,
    )
```

time: 386 us -> 60.8 us (0.16)
  the two profiles are of different devices: /device:TPU:33 before, /device:TPU:6 now
where the time goes in v1:
time: 60.8 us; the launch traced here: 60.5 us
  Pallas kernels  55.5 us (91%)
  local copies, waits for them, and re-layouts  4.39 us (7%)
  between operations  0.66 us (1%)
    pallas_call x1, Pallas kernels, local(): pl.pallas_call(functools.partial(section, sizes), out_shape=(jax.ShapeDty...  43.2 us
    pallas_call x1, Pallas kernels, local(): pl.pallas_call(functools.partial(finish, 1.0 / math.sqrt(ni * li * nj * l...  12.2 us
    unnamed x12, local copies, waits for them, and re-layouts  4.39 us

profile of v1, /device:TPU:6, one launch (start us, length us, event | category | flops | bytes accessed | tf_op | source)
XLA Modules:
  0.0 60.5 jit_solution(10733035389637181402)
XLA Ops:
  0.6 0.0 copy-start
  0.6 1.0 %copy-done = f32[8,5,16,128]{3,2,1,0:T(8,128)S(1)} copy-done((f32[8,5,16,128]{3,2,1,0:T(8,128)S(1)}, f32[8,5,16,128]{3,2,1,0:T(8,128)}, u32[]{:S(2)}) %copy-start) | copy-done | bytes 327704
  1.6 0.0 copy-start.2
  1.6 0.8 %copy-done.2 = f32[8,8,16]{2,1,0:T(8,128)S(1)} copy-done((f32[8,8,16]{2,1,0:T(8,128)S(1)}, f32[8,8,16]{2,1,0:T(8,128)}, u32[]{:S(2)}) %copy-start.2) | copy-done | bytes 4120
  2.4 0.0 copy-start.3
  2.4 0.7 %copy-done.3 = s32[8,16]{1,0:T(8,128)S(1)} copy-done((s32[8,16]{1,0:T(8,128)S(1)}, s32[8,16]{1,0:T(8,128)}, u32[]{:S(2)}) %copy-start.3) | copy-done | bytes 536
  3.0 0.0 copy-start.5
  3.1 0.7 %copy-done.5 = f32[2,64]{1,0:T(2,128)S(1)} copy-done((f32[2,64]{1,0:T(2,128)S(1)}, f32[2,64]{1,0:T(2,128)}, u32[]{:S(2)}) %copy-start.5) | copy-done | bytes 536
  3.7 43.2 %section.1 = (f32[8,5,16,128]{3,2,1,0:T(8,128)S(1)}, f32[8,128]{1,0:T(8,128)S(1)}) custom-call(f32[8,5,16,128]{3,2,1,0:T(8,128)S(1)} %copy-done, f32[8,8,16]{2,1,0:T(8,128)S(1)} %copy-done.2, f32[2,64]{1,0:T(2,128)S(1)} %copy-done.5, s32[8,16]{1,0:T(8,128)S(1)} %copy-done.3), custom_call_target="tpu_custom_call" | custom-call | tf_op jit(solution)/shard_map/section/pallas_call | solution.py:422
  47.0 0.0 copy-start.1
  47.0 0.7 %copy-done.1 = f32[8,5,16,128]{3,2,1,0:T(8,128)} copy-done((f32[8,5,16,128]{3,2,1,0:T(8,128)}, f32[8,5,16,128]{3,2,1,0:T(8,128)S(1)}, u32[]{:S(2)}) %copy-start.1) | copy-done | bytes 327704
  47.7 0.0 copy-start.4
  47.7 0.6 copy-done.4
  48.3 12.2 %finish.1 = (f32[8,5,16,128]{3,2,1,0:T(8,128)}, f32[1,8]{1,0:T(1,128)}) custom-call(f32[8,5,16,128]{3,2,1,0:T(8,128)} %copy-done.1, f32[8,128]{1,0:T(8,128)} %copy-done.4), custom_call_target="tpu_custom_call" | custom-call | tf_op jit(solution)/shard_map/finish/pallas_call | solution.py:459
Async XLA Ops:
  0.6 1.0 %copy-start = (f32[8,5,16,128]{3,2,1,0:T(8,128)S(1)}, f32[8,5,16,128]{3,2,1,0:T(8,128)}, u32[]{:S(2)}) copy-start(f32[8,5,16,128]{3,2,1,0:T(8,128)} %flow.1) | copy-start | bytes 983044
  1.6 0.8 %copy-start.2 = (f32[8,8,16]{2,1,0:T(8,128)S(1)}, f32[8,8,16]{2,1,0:T(8,128)}, u32[]{:S(2)}) copy-start(f32[8,8,16]{2,1,0:T(8,128)} %shapes.1) | copy-start | bytes 12292
  2.4 0.7 %copy-start.3 = (s32[8,16]{1,0:T(8,128)S(1)}, s32[8,16]{1,0:T(8,128)}, u32[]{:S(2)}) copy-start(s32[8,16]{1,0:T(8,128)} %mask.1) | copy-start | bytes 1540
  3.0 0.7 %copy-start.5 = (f32[2,64]{1,0:T(2,128)S(1)}, f32[2,64]{1,0:T(2,128)}, u32[]{:S(2)}) copy-start(f32[2,64]{1,0:T(2,128)} %coords.1) | copy-start | bytes 1540
  47.0 0.7 %copy-start.1 = (f32[8,5,16,128]{3,2,1,0:T(8,128)}, f32[8,5,16,128]{3,2,1,0:T(8,128)S(1)}, u32[]{:S(2)}) copy-start(f32[8,5,16,128]{3,2,1,0:T(8,128)S(1)} %get-tuple-element.6.new) | copy-start | bytes 983044
  47.7 0.6 copy-start.4

commit v2 on v1

--- a/solution.py
+++ b/solution.py
@@ -56,8 +56,8 @@
 
 
 def section(
-    sizes, flow, shapes, coords, mask, new, force,
-    fv, sv, mv, prim, raw_i, raw_j, send_k, halo_k, edge_k, planes, planes_in,
+    sizes, flow, shapes, coords_in, mask, new, force,
+    fv, sv, mv, coords, prim, raw_i, raw_j, send_k, halo_k, edge_k, planes, planes_in,
     s_own, l_own, s_all, l_all, g_own, g_in, flux_i,
     local_sem, send_sem, recv_sem, many_sem,
 ):
@@ -73,9 +73,11 @@
     in_flow = pltpu.make_async_copy(flow, fv, local_sem.at[0])
     in_shapes = pltpu.make_async_copy(shapes, sv, local_sem.at[1])
     in_mask = pltpu.make_async_copy(mask, mv, local_sem.at[2])
+    in_coords = pltpu.make_async_copy(coords_in, coords, local_sem.at[3])
     in_flow.start()
     in_shapes.start()
     in_mask.start()
+    in_coords.start()
 
     barrier = pltpu.get_barrier_semaphore()
 
@@ -112,14 +114,16 @@
 
     in_shapes.wait()
     in_mask.wait()
-    packed = jnp.zeros((li, 128), jnp.float32)
+    in_coords.wait()
+    packed = jnp.zeros((modes, 128), jnp.float32)
     disp = jnp.zeros((li, lj), jnp.float32)
     speed = jnp.zeros((li, lj), jnp.float32)
-    zeros = jnp.zeros((li, 128 - lj), jnp.float32)
+    zeros = jnp.zeros((modes, 128 - lj), jnp.float32)
+    for i in range(li):
+        wide = jnp.concatenate([sv[:, i, :], zeros], axis=1)
+        packed = packed + (pltpu.roll(wide, lj * i, 1) if i else wide)
     for m in range(modes):
         one = sv[m]
-        wide = jnp.concatenate([one, zeros], axis=1)
-        packed = packed + (pltpu.roll(wide, lj * m, 1) if m else wide)
         disp = disp + coords[0, ka * modes + m] * one
         speed = speed + coords[1, ka * modes + m] * one
     s_own[...] = packed
@@ -136,7 +140,8 @@
             turned = turned + jnp.where(lax.rem(lane_t, li) == i, p - FAR_PRESSURE, 0.0)
         flat = jnp.concatenate([turned] * (128 // lj), axis=0).T[0:li]
         keep = jnp.concatenate([mv[...]] * (128 // lj), axis=1)
-        l_own[...] = jnp.where(keep == 1, flat, 0.0)
+        own_row = lane // lj == lax.broadcasted_iota(jnp.int32, (8, 128), 0)
+        l_own[...] = jnp.sum(jnp.where(own_row & (keep == 1), flat, 0.0), axis=0, keepdims=True)
 
     pl.semaphore_wait(barrier, expected)
 
@@ -359,7 +364,10 @@
         def _():
             pltpu.make_async_copy(l_all, l_all, many_sem.at[1]).wait()
 
-        g_own[...] = jnp.sum(s_all[...] * l_all[...], axis=0)
+        summed = jnp.sum(s_all[...] * l_all[...], axis=0)
+        each = jnp.sum(summed, axis=1, keepdims=True)
+        row = lax.broadcasted_iota(jnp.int32, (8, 128), 0)
+        g_own[...] = jnp.sum(jnp.where(lane == row, each, 0.0), axis=0, keepdims=True)
 
         @pl.loop(1, columns)
         def _(c):
@@ -391,19 +399,14 @@
 
     @pl.when(is_root)
     def _():
-        others = s_all.at[1:columns]
+        others = l_all.at[1:columns]
         pltpu.make_async_copy(others, others, many_sem.at[4]).wait()
 
 
 def finish(scale, new, partial, out, force, sem):
     copy = pltpu.make_async_copy(new, out, sem)
     copy.start()
-    group = partial.shape[1] // 8
-    row = lax.broadcasted_iota(jnp.int32, (8, 128), 0)
-    lane = lax.broadcasted_iota(jnp.int32, (8, 128), 1)
-    summed = jnp.sum(partial[...], axis=0, keepdims=True)
-    each = jnp.sum(jnp.where(lane // group == row, summed, 0.0), axis=1, keepdims=True)
-    force[...] = jnp.sum(jnp.where(lane == row, each, 0.0), axis=0, keepdims=True)[:, 0:8] * scale
+    force[...] = partial[:, 0 : force.shape[1]] * scale
     copy.wait()
 
 
@@ -416,21 +419,20 @@
         modes = mode_shapes.shape[0]
         f32 = jnp.float32
         tile = pltpu.VMEM((8, 128), f32)
+        row = pltpu.VMEM((1, 128), f32)
         vmem = pl.BlockSpec(memory_space=pltpu.VMEM)
         hbm = pl.BlockSpec(memory_space=pltpu.HBM)
-        free = pl.BlockSpec(memory_space=pl.ANY)
+        held = functools.partial(pltpu.with_memory_space_constraint, memory_space=pltpu.HBM)
         new, partial = pl.pallas_call(
             functools.partial(section, sizes),
-            out_shape=(
-                jax.ShapeDtypeStruct(flow_state.shape, f32),
-                jax.ShapeDtypeStruct((8, 128), f32),
-            ),
-            in_specs=[hbm, hbm, pl.BlockSpec(memory_space=pltpu.SMEM), hbm],
+            out_shape=(pltpu.VMEM(flow_state.shape, f32), pltpu.VMEM((1, 128), f32)),
+            in_specs=[hbm, hbm, hbm, hbm],
             out_specs=(vmem, vmem),
             scratch_shapes=[
                 pltpu.VMEM(flow_state.shape, f32),
                 pltpu.VMEM(mode_shapes.shape, f32),
                 pltpu.VMEM(wall_mask.shape, jnp.int32),
+                pltpu.SMEM(modal_coords.shape, f32),
                 pltpu.VMEM((li + 4, 5, lj + 24, lk), f32),
                 pltpu.VMEM((2, 2, 5, lj, lk), f32),
                 pltpu.VMEM((2, li, 5, 8, lk), f32),
@@ -440,13 +442,13 @@
                 tile,
                 pltpu.VMEM((nk - 1, 8, 128), f32),
                 tile,
-                tile,
+                row,
                 pltpu.VMEM((ni * nj, 8, 128), f32),
-                pltpu.VMEM((ni * nj, 8, 128), f32),
-                tile,
-                tile,
+                pltpu.VMEM((ni * nj, 1, 128), f32),
+                row,
+                row,
                 pltpu.VMEM((5, lj, lk), f32),
-                pltpu.SemaphoreType.DMA((3,)),
+                pltpu.SemaphoreType.DMA((4,)),
                 pltpu.SemaphoreType.DMA((15 + nk,)),
                 pltpu.SemaphoreType.DMA((6,)),
                 pltpu.SemaphoreType.DMA((5,)),
@@ -455,16 +457,17 @@
                 collective_id=0, has_side_effects=True, vmem_limit_bytes=32 * 1024 * 1024
             ),
             name="section",
-        )(flow_state, mode_shapes, modal_coords, wall_mask)
+        )(held(flow_state), held(mode_shapes), held(modal_coords), held(wall_mask))
         out, force = pl.pallas_call(
             functools.partial(finish, 1.0 / math.sqrt(ni * li * nj * lj)),
             out_shape=(
                 jax.ShapeDtypeStruct(flow_state.shape, f32),
                 jax.ShapeDtypeStruct((1, modes), f32),
             ),
-            in_specs=[free, vmem],
+            in_specs=[vmem, vmem],
             out_specs=(hbm, vmem),
             scratch_shapes=[pltpu.SemaphoreType.DMA],
+            compiler_params=pltpu.CompilerParams(vmem_limit_bytes=8 * 1024 * 1024),
             name="finish",
         )(new, partial)
         return (out, force.reshape(modes))

time: 60.8 us -> 32.3 us (0.53)
  Pallas kernels: 55.5 us -> 31.2 us
  local copies, waits for them, and re-layouts: 4.39 us -> 0 us
    pallas_call x1, Pallas kernels: 43.2 us -> 30 us  [local(): pl.pallas_call(functools.partial(section, sizes), out_shape=(pltpu.VMEM(f...]
    pallas_call x1, Pallas kernels: 12.2 us -> 1.24 us  [local(): pl.pallas_call(functools.partial(finish, 1.0 / math.sqrt(ni * li * nj * l...]
    unnamed x12 -> x0, local copies, waits for them, and re-layouts: 4.39 us -> none
where the time goes in v2:
time: 32.3 us; the launch traced here: 31.9 us
  Pallas kernels  31.2 us (97%)
  between operations  0.64 us (2%)
    pallas_call x1, Pallas kernels, local(): pl.pallas_call(functools.partial(section, sizes), out_shape=(pltpu.VMEM(f...  30 us
    pallas_call x1, Pallas kernels, local(): pl.pallas_call(functools.partial(finish, 1.0 / math.sqrt(ni * li * nj * l...  1.24 us

profile of v2, /device:TPU:6, one launch (start us, length us, event | category | flops | bytes accessed | tf_op | source)
XLA Modules:
  0.0 31.9 jit_solution(6754693081624785615)
XLA Ops:
  0.6 30.0 %section.1 = (f32[8,5,16,128]{3,2,1,0:T(8,128)S(1)}, f32[1,128]{1,0:T(1,128)S(1)}) custom-call(f32[8,5,16,128]{3,2,1,0:T(8,128)} %flow.1, f32[8,8,16]{2,1,0:T(8,128)} %shapes.1, f32[2,64]{1,0:T(2,128)} %coords_in.1, s32[8,16]{1,0:T(8,128)} %mask.1), custom_call_target="tpu_custom_call" | custom-call | tf_op jit(solution)/shard_map/section/pallas_call | solution.py:426
  30.6 1.2 %finish.1 = (f32[8,5,16,128]{3,2,1,0:T(8,128)}, f32[1,8]{1,0:T(1,128)}) custom-call(f32[8,5,16,128]{3,2,1,0:T(8,128)S(1)} %get-tuple-element.6.new, f32[1,128]{1,0:T(1,128)S(1)} %get-tuple-element.7.partial), custom_call_target="tpu_custom_call" | custom-call | tf_op jit(solution)/shard_map/finish/pallas_call | solution.py:461

commit v3 on v2

--- a/solution.py
+++ b/solution.py
@@ -12,6 +12,8 @@
 SECTION_STEP = 0.2
 STRAIN = 0.25
 FAR_PRESSURE = 0.8
+ROOT_WALL = (1, 0)
+ROOT = (0, 0)
 FAR_STATE = (1.0, 0.6, 0.0, 0.0, 0.8)
 
 
@@ -58,16 +60,20 @@
 def section(
     sizes, flow, shapes, coords_in, mask, new, force,
     fv, sv, mv, coords, prim, raw_i, raw_j, send_k, halo_k, edge_k, planes, planes_in,
-    s_own, l_own, s_all, l_all, g_own, g_in, flux_i,
-    local_sem, send_sem, recv_sem, many_sem,
+    s_own, l_own, s_all, l_all, g_own, flux_i,
+    local_sem, send_sem, recv_sem, many_sem, column_sem,
 ):
     ni, nj, nk = sizes
     ia, ja, ka = lax.axis_index("ia"), lax.axis_index("ja"), lax.axis_index("ka")
     li, lj, lk = flow.shape[0], flow.shape[2], flow.shape[3]
     modes = shapes.shape[0]
     columns = ni * nj
+    lines = 8 if ni % 8 == 0 else ni
+    root_of = [(i % lines, j % nj) for i, j in [ROOT_WALL] + [ROOT] * (nk - 1)]
+    root_ia = jnp.where(ka == 0, root_of[0][0], root_of[-1][0])
+    root_ja = jnp.where(ka == 0, root_of[0][1], root_of[-1][1])
     column = ia * nj + ja
-    is_root = column == 0
+    is_root = column == root_ia * nj + root_ja
     total_k = nk * lk
 
     in_flow = pltpu.make_async_copy(flow, fv, local_sem.at[0])
@@ -86,15 +92,19 @@
 
     @pl.when(is_root)
     def _():
+        def next_to(c):
+            c = lax.rem(2 * columns - c + column, columns)
+            return {"ia": c // nj, "ja": lax.rem(c, nj)}
+
+        @pl.when(ka > 0)
+        def _():
+            @pl.loop(0, columns)
+            def _(c):
+                greet({**next_to(c), "ka": 0})
+
         @pl.loop(1, columns)
         def _(c):
-            greet({"ia": c // nj, "ja": lax.rem(c, nj)})
-
-        @pl.when(ka > 0)
-        def _():
-            @pl.loop(0, columns)
-            def _(c):
-                greet({"ia": c // nj, "ja": lax.rem(c, nj), "ka": 0})
+            greet(next_to(c))
 
     beside = [
         (ia > 0, {"ia": jnp.maximum(ia - 1, 0)}),
@@ -102,13 +112,14 @@
         (ja > 0, {"ja": jnp.maximum(ja - 1, 0)}),
         (ja < nj - 1, {"ja": jnp.minimum(ja + 1, nj - 1)}),
     ]
-    expected = nk - 1
+    expected = jnp.where(is_root, 0, 1) + jnp.where(ka == 0, nk - 1, 0)
     for there, where in beside:
         pl.when(there)(functools.partial(greet, where))
         expected = expected + there.astype(jnp.int32)
-    for o in range(1, nk):
-        greet({"ka": lax.rem(ka + o, nk)})
-    expected = expected + jnp.where(is_root, 0, 1) + jnp.where(ka == 0, nk - 1, 0)
+    lead = nk // 2
+    leads = ka == lead
+    pl.when(~leads)(functools.partial(greet, {"ka": lead}))
+    expected = expected + jnp.where(leads, nk - 1, 0)
 
     lane = lax.broadcasted_iota(jnp.int32, (8, 128), 1)
 
@@ -145,18 +156,26 @@
 
     pl.semaphore_wait(barrier, expected)
 
+    @pl.when(leads)
+    def _():
+        for o in range(1, nk):
+            pl.semaphore_signal(
+                column_sem, inc=1, device_id={"ka": lax.rem(ka + o, nk)}, device_id_type=MESH
+            )
+
     def to_root(src, dst, sem_index, recv, where):
         return pltpu.make_async_remote_copy(
             src_ref=src, dst_ref=dst, send_sem=send_sem.at[sem_index], recv_sem=recv,
             device_id=where, device_id_type=MESH,
         )
 
-    root_here = {"ia": 0, "ja": 0}
+    slots = [lax.rem(column - (i * nj + j) + columns, columns) for i, j in root_of]
     load_copies = [
-        to_root(l_own, l_all.at[column], 8 + o, many_sem.at[1], {"ia": 0, "ja": 0, "ka": o})
+        to_root(l_own, l_all.at[slots[o]], 8 + o, many_sem.at[1], {"ia": root_of[o][0], "ja": root_of[o][1], "ka": o})
         for o in range(nk)
     ]
-    shape_copy = to_root(s_own, s_all.at[column], 7, many_sem.at[0], root_here)
+    slot = jnp.where(ka == 0, slots[0], slots[-1])
+    shape_copy = to_root(s_own, s_all.at[slot], 7, many_sem.at[0], {"ia": root_ia, "ja": root_ja})
 
     @pl.when(ka == 0)
     def _():
@@ -187,8 +206,8 @@
     copies = [
         (halo(flow.at[li - 2 : li], raw_i.at[0], 0, to_i1), has_i1, has_i0),
         (halo(flow.at[0:2], raw_i.at[1], 1, to_i0), has_i0, has_i1),
-        (halo(flow.at[:, :, lj - 8 : lj], raw_j.at[0], 2, to_j1), has_j1, has_j0),
-        (halo(flow.at[:, :, 0:8], raw_j.at[1], 3, to_j0), has_j0, has_j1),
+        (halo(flow.at[:, :, lj - 2 : lj], raw_j.at[0, :, :, 6:8], 2, to_j1), has_j1, has_j0),
+        (halo(flow.at[:, :, 0:2], raw_j.at[1, :, :, 0:2], 3, to_j0), has_j0, has_j1),
         (halo(send_k.at[0], halo_k.at[0], 4, {"ka": jnp.minimum(ka + 1, nk - 1)}), has_k1, has_k0),
         (halo(send_k.at[1], halo_k.at[1], 5, {"ka": jnp.maximum(ka - 1, 0)}), has_k0, has_k1),
     ]
@@ -202,9 +221,6 @@
         )
         for o in range(1, nk)
     ]
-    for copy in plane_copies:
-        copy.start()
-
     lane_j = lax.broadcasted_iota(jnp.int32, (lj, 128), 1)
     send_k[...] = jnp.zeros_like(send_k)
 
@@ -216,11 +232,40 @@
             send_k[0, c] = jnp.where(here, pltpu.roll(w, 2 * i + 2, 1), send_k[0, c])
             send_k[1, c] = jnp.where(here, pltpu.roll(w, 2 * i, 1), send_k[1, c])
 
+    def far(shape, c):
+        return jnp.full(shape, FAR_STATE[c], jnp.float32)
+
+    for base, (_, _, gets) in zip((0, li + 2), copies[0:2]):
+
+        @pl.when(~gets)
+        def _(base=base):
+            for r in range(2):
+                for c in range(5):
+                    prim[base + r, c, 8 : 8 + lj] = far((lj, lk), c)
+
+    for base, (_, _, gets) in zip((0, 8 + lj), copies[2:4]):
+
+        @pl.when(~gets)
+        def _(base=base):
+            @pl.loop(0, li)
+            def _(i):
+                for c in range(5):
+                    prim[i + 2, c, base : base + 8] = far((8, lk), c)
+
+    @pl.when(~has_k0)
+    def _():
+        halo_k[0] = jnp.zeros(halo_k.shape[1:], jnp.float32)
+
+    @pl.when(~has_k1)
+    def _():
+        for c in range(5):
+            halo_k[1, c] = far((lj, 128), c)
+
+    pl.when(~leads)(functools.partial(pl.semaphore_wait, column_sem, 1))
+    for copy in plane_copies:
+        copy.start()
     for copy, sends, _ in copies[4:6]:
         pl.when(sends)(copy.start)
-
-    def far(shape, c):
-        return jnp.full(shape, FAR_STATE[c], jnp.float32)
 
     pltpu.make_async_copy(planes_in, planes_in, many_sem.at[2]).wait()
     total = planes[...]
@@ -230,21 +275,6 @@
     wall = jnp.concatenate([jnp.zeros((li, 2 * lj), jnp.float32), wall, jnp.zeros((li, 128 - 3 * lj), jnp.float32)], axis=1)
     turned = jnp.concatenate([total + wall, jnp.zeros((128 - li, 128), jnp.float32)], axis=0).T
 
-    for side, (base, (copy, _, gets)) in enumerate(zip((0, li + 2), copies[0:2])):
-
-        @pl.when(gets)
-        def _(side=side, base=base, copy=copy):
-            copy.wait_recv()
-            for r in range(2):
-                for c, w in enumerate(primitives([raw_i[side, r, c] for c in range(5)])):
-                    prim[base + r, c, 8 : 8 + lj] = w
-
-        @pl.when(~gets)
-        def _(base=base):
-            for r in range(2):
-                for c in range(5):
-                    prim[base + r, c, 8 : 8 + lj] = far((lj, lk), c)
-
     for side, (base, (copy, _, gets)) in enumerate(zip((0, 8 + lj), copies[2:4])):
 
         @pl.when(gets)
@@ -256,24 +286,8 @@
                 for c, w in enumerate(primitives([raw_j[side, i, c] for c in range(5)])):
                     prim[i + 2, c, base : base + 8] = w
 
-        @pl.when(~gets)
-        def _(base=base):
-            @pl.loop(0, li)
-            def _(i):
-                for c in range(5):
-                    prim[i + 2, c, base : base + 8] = far((8, lk), c)
-
     pl.when(has_k0)(copies[4][0].wait_recv)
     pl.when(has_k1)(copies[5][0].wait_recv)
-
-    @pl.when(~has_k0)
-    def _():
-        halo_k[0] = jnp.zeros(halo_k.shape[1:], jnp.float32)
-
-    @pl.when(~has_k1)
-    def _():
-        for c in range(5):
-            halo_k[1, c] = far((lj, 128), c)
 
     first = ka * lk
     own_pair = [send_k[0, c] for c in range(5)]
@@ -299,8 +313,6 @@
     def along_i(i):
         return faces(cells(i, 8, lj), cells(i + 1, 8, lj), cells(i + 2, 8, lj), cells(i + 3, 8, lj), 1)
 
-    for c, w in enumerate(along_i(0)):
-        flux_i[c] = w
     at_wall = ka == 0
     lane_f = (first + lane_j).astype(jnp.float32)
     face_weight = (1.0 - lane_f / total_k) ** 2
@@ -309,7 +321,22 @@
     column_lane = lax.broadcasted_iota(jnp.int32, (3 * lj, 128), 1)
 
     @pl.loop(0, li)
-    def _(i):
+    def _(n):
+        i = jnp.where(n < li - 4, n + 2, jnp.where(n < li - 2, n - (li - 4), n))
+        for side, (turn, base) in enumerate(((li - 4, 0), (li - 2, li + 2))):
+
+            @pl.when((n == turn) & copies[side][2])
+            def _(side=side, base=base):
+                copies[side][0].wait_recv()
+                for r in range(2):
+                    for c, w in enumerate(primitives([raw_i[side, r, c] for c in range(5)])):
+                        prim[base + r, c, 8 : 8 + lj] = w
+
+        @pl.when((n == 0) | (n == li - 4) | (n == li - 2))
+        def _():
+            for c, w in enumerate(along_i(i)):
+                flux_i[c] = w
+
         column_i = jnp.sum(jnp.where(column_lane == i, turned[0 : 3 * lj], 0.0), axis=1, keepdims=True)
         disp_i = column_i[0:lj]
         speed_i = jnp.broadcast_to(column_i[lj : 2 * lj], (lj, 128))
@@ -350,39 +377,6 @@
             high = jnp.where(last_lane, end, pltpu.roll(f, lk - 1, 1))
             new[i, c] = fv[i, c] + growth * (residual[c] + (high - f))
 
-    @pl.when(is_root)
-    def _():
-        others = s_all.at[1:columns]
-        pltpu.make_async_copy(others, others, many_sem.at[0]).wait()
-
-        @pl.when(ka == 0)
-        def _():
-            loads = l_all.at[1:columns]
-            pltpu.make_async_copy(loads, loads, many_sem.at[1]).wait()
-
-        @pl.when(ka > 0)
-        def _():
-            pltpu.make_async_copy(l_all, l_all, many_sem.at[1]).wait()
-
-        summed = jnp.sum(s_all[...] * l_all[...], axis=0)
-        each = jnp.sum(summed, axis=1, keepdims=True)
-        row = lax.broadcasted_iota(jnp.int32, (8, 128), 0)
-        g_own[...] = jnp.sum(jnp.where(lane == row, each, 0.0), axis=0, keepdims=True)
-
-        @pl.loop(1, columns)
-        def _(c):
-            pltpu.make_async_remote_copy(
-                src_ref=g_own, dst_ref=g_in, send_sem=many_sem.at[4], recv_sem=many_sem.at[3],
-                device_id={"ia": c // nj, "ja": lax.rem(c, nj)}, device_id_type=MESH,
-            ).start()
-
-        force[...] = g_own[...]
-
-    @pl.when(~is_root)
-    def _():
-        pltpu.make_async_copy(g_in, g_in, many_sem.at[3]).wait()
-        force[...] = g_in[...]
-
     for copy, sends, _ in copies:
         pl.when(sends)(copy.wait_send)
     for copy in plane_copies:
@@ -397,10 +391,71 @@
             else:
                 pl.when(~is_root)(copy.wait_send)
 
+    near = min(3, nj)
+    line = lax.rem(ia, lines)
+    order = sorted(range(lines), key=lambda o: min(o, lines - o))
+    direct = [
+        {"ia": lax.rem(root_ia + o, lines), "ja": lax.rem(root_ja + j, near)}
+        for j in range(near)
+        for o in order
+        if j or o
+    ]
+    passed = [
+        {"ia": line + lines * h, "ja": j}
+        for h in range(ni // lines)
+        for j in range(nj)
+        if h or j >= near
+    ]
+    hands_on = (ia < lines) & (ja == jnp.where((line == root_ia) & (root_ja == 0), min(1, nj - 1), 0))
+
+    def give(targets):
+        for where in targets:
+            pltpu.make_async_remote_copy(
+                src_ref=g_own, dst_ref=g_own, send_sem=many_sem.at[4], recv_sem=many_sem.at[3],
+                device_id=where, device_id_type=MESH,
+            ).start()
+
+    def sent(targets):
+        if targets:
+            left = l_all.at[0 : len(targets)]
+            pltpu.make_async_copy(left, left, many_sem.at[4]).wait()
+
     @pl.when(is_root)
     def _():
-        others = l_all.at[1:columns]
-        pltpu.make_async_copy(others, others, many_sem.at[4]).wait()
+        others = s_all.at[1:columns]
+        pltpu.make_async_copy(others, others, many_sem.at[0]).wait()
+
+        @pl.when(ka == 0)
+        def _():
+            loads = l_all.at[1:columns]
+            pltpu.make_async_copy(loads, loads, many_sem.at[1]).wait()
+
+        @pl.when(ka > 0)
+        def _():
+            pltpu.make_async_copy(l_all, l_all, many_sem.at[1]).wait()
+
+        summed = jnp.sum(s_all[...] * l_all[...], axis=0)
+        each = jnp.sum(summed, axis=1, keepdims=True)
+        row = lax.broadcasted_iota(jnp.int32, (8, 128), 0)
+        g_own[...] = jnp.sum(jnp.where(lane == row, each, 0.0), axis=0, keepdims=True)
+
+        give(direct)
+        force[...] = g_own[...]
+        sent(direct)
+
+    @pl.when(~is_root)
+    def _():
+        pltpu.make_async_copy(g_own, g_own, many_sem.at[3]).wait()
+
+        @pl.when(hands_on)
+        def _():
+            give(passed)
+
+        force[...] = g_own[...]
+
+        @pl.when(hands_on)
+        def _():
+            sent(passed)
 
 
 def finish(scale, new, partial, out, force, sem):
@@ -446,12 +501,12 @@
                 pltpu.VMEM((ni * nj, 8, 128), f32),
                 pltpu.VMEM((ni * nj, 1, 128), f32),
                 row,
-                row,
                 pltpu.VMEM((5, lj, lk), f32),
                 pltpu.SemaphoreType.DMA((4,)),
                 pltpu.SemaphoreType.DMA((15 + nk,)),
                 pltpu.SemaphoreType.DMA((6,)),
                 pltpu.SemaphoreType.DMA((5,)),
+                pltpu.SemaphoreType.REGULAR,
             ],
             compiler_params=pltpu.CompilerParams(
                 collective_id=0, has_side_effects=True, vmem_limit_bytes=32 * 1024 * 1024

time: 32.3 us -> 29.4 us (0.910)
  the two profiles are of different devices: /device:TPU:6 before, /device:TPU:40 now
where the time goes in v3:
time: 29.4 us; the launch traced here: 29.2 us
  Pallas kernels  28.6 us (97%)
  between operations  0.64 us (2%)
    pallas_call x1, Pallas kernels, local(): pl.pallas_call(functools.partial(section, sizes), out_shape=(pltpu.VMEM(f...  27.3 us
    pallas_call x1, Pallas kernels, local(): pl.pallas_call(functools.partial(finish, 1.0 / math.sqrt(ni * li * nj * l...  1.24 us

profile of v3, /device:TPU:40, one launch (start us, length us, event | category | flops | bytes accessed | tf_op | source)
XLA Modules:
  0.0 29.2 jit_solution(14077901635765483538)
XLA Ops:
  0.6 27.3 %section.1 = (f32[8,5,16,128]{3,2,1,0:T(8,128)S(1)}, f32[1,128]{1,0:T(1,128)S(1)}) custom-call(f32[8,5,16,128]{3,2,1,0:T(8,128)} %flow.1, f32[8,8,16]{2,1,0:T(8,128)} %shapes.1, f32[2,64]{1,0:T(2,128)} %coords_in.1, s32[8,16]{1,0:T(8,128)} %mask.1), custom_call_target="tpu_custom_call" | custom-call | tf_op jit(solution)/shard_map/section/pallas_call | solution.py:481
  28.0 1.2 %finish.1 = (f32[8,5,16,128]{3,2,1,0:T(8,128)}, f32[1,8]{1,0:T(1,128)}) custom-call(f32[8,5,16,128]{3,2,1,0:T(8,128)S(1)} %get-tuple-element.6.new, f32[1,128]{1,0:T(1,128)S(1)} %get-tuple-element.7.partial), custom_call_target="tpu_custom_call" | custom-call | tf_op jit(solution)/shard_map/finish/pallas_call | solution.py:516

commit v4 on v3

--- a/solution.py
+++ b/solution.py
@@ -391,9 +391,9 @@
             else:
                 pl.when(~is_root)(copy.wait_send)
 
-    near = min(3, nj)
+    near = min(4, nj)
     line = lax.rem(ia, lines)
-    order = sorted(range(lines), key=lambda o: min(o, lines - o))
+    order = [o % lines for o in (1, 4, 5, 2, 3, 6, 7, 0)][:lines] if lines == 8 else list(range(lines))
     direct = [
         {"ia": lax.rem(root_ia + o, lines), "ja": lax.rem(root_ja + j, near)}
         for j in range(near)
@@ -406,7 +406,7 @@
         for j in range(nj)
         if h or j >= near
     ]
-    hands_on = (ia < lines) & (ja == jnp.where((line == root_ia) & (root_ja == 0), min(1, nj - 1), 0))
+    hands_on = (ia < lines) & (ja == near - 1)
 
     def give(targets):
         for where in targets:

time: 29.4 us -> 28 us (0.952)
  Pallas kernels: 28.6 us -> 27.2 us
    pallas_call x1, Pallas kernels: 27.3 us -> 26 us  [local(): pl.pallas_call(functools.partial(section, sizes), out_shape=(pltpu.VMEM(f...]
where the time goes in v4:
time: 28 us; the launch traced here: 27.8 us
  Pallas kernels  27.2 us (97%)
  between operations  0.64 us (2%)
    pallas_call x1, Pallas kernels, local(): pl.pallas_call(functools.partial(section, sizes), out_shape=(pltpu.VMEM(f...  26 us
    pallas_call x1, Pallas kernels, local(): pl.pallas_call(functools.partial(finish, 1.0 / math.sqrt(ni * li * nj * l...  1.24 us

profile of v4, /device:TPU:40, one launch (start us, length us, event | category | flops | bytes accessed | tf_op | source)
XLA Modules:
  0.0 27.8 jit_solution(13257492131107337300)
XLA Ops:
  0.6 26.0 %section.1 = (f32[8,5,16,128]{3,2,1,0:T(8,128)S(1)}, f32[1,128]{1,0:T(1,128)S(1)}) custom-call(f32[8,5,16,128]{3,2,1,0:T(8,128)} %flow.1, f32[8,8,16]{2,1,0:T(8,128)} %shapes.1, f32[2,64]{1,0:T(2,128)} %coords_in.1, s32[8,16]{1,0:T(8,128)} %mask.1), custom_call_target="tpu_custom_call" | custom-call | tf_op jit(solution)/shard_map/section/pallas_call | solution.py:481
  26.6 1.2 %finish.1 = (f32[8,5,16,128]{3,2,1,0:T(8,128)}, f32[1,8]{1,0:T(1,128)}) custom-call(f32[8,5,16,128]{3,2,1,0:T(8,128)S(1)} %get-tuple-element.6.new, f32[1,128]{1,0:T(1,128)S(1)} %get-tuple-element.7.partial), custom_call_target="tpu_custom_call" | custom-call | tf_op jit(solution)/shard_map/finish/pallas_call | solution.py:516

commit v5 on v4

--- a/solution.py
+++ b/solution.py
@@ -12,8 +12,6 @@
 SECTION_STEP = 0.2
 STRAIN = 0.25
 FAR_PRESSURE = 0.8
-ROOT_WALL = (1, 0)
-ROOT = (0, 0)
 FAR_STATE = (1.0, 0.6, 0.0, 0.0, 0.8)
 
 
@@ -60,7 +58,7 @@
 def section(
     sizes, flow, shapes, coords_in, mask, new, force,
     fv, sv, mv, coords, prim, raw_i, raw_j, send_k, halo_k, edge_k, planes, planes_in,
-    s_own, l_own, s_all, l_all, g_own, flux_i,
+    s_own, l_own, s_all, l_all, g_sum, g_own, flux_i,
     local_sem, send_sem, recv_sem, many_sem, column_sem,
 ):
     ni, nj, nk = sizes
@@ -69,11 +67,15 @@
     modes = shapes.shape[0]
     columns = ni * nj
     lines = 8 if ni % 8 == 0 else ni
-    root_of = [(i % lines, j % nj) for i, j in [ROOT_WALL] + [ROOT] * (nk - 1)]
-    root_ia = jnp.where(ka == 0, root_of[0][0], root_of[-1][0])
-    root_ja = jnp.where(ka == 0, root_of[0][1], root_of[-1][1])
+    root_of = [(1 - o % 2, o + 1 - o % 2) for o in range(nk)]
+    odd = lax.rem(ka, 2) == 1
+    root_ia = jnp.where(odd, 0, 1)
+    root_ka = jnp.where(odd, ka, ka + 1 - lax.rem(ka, 2))
     column = ia * nj + ja
-    is_root = column == root_ia * nj + root_ja
+    own_root = odd & (column == 0)
+    other_root = odd & (column == nj)
+    is_root = own_root | other_root
+    serves = jnp.where(own_root, ka, jnp.maximum(ka - 1, 0))
     total_k = nk * lk
 
     in_flow = pltpu.make_async_copy(flow, fv, local_sem.at[0])
@@ -96,15 +98,17 @@
             c = lax.rem(2 * columns - c + column, columns)
             return {"ia": c // nj, "ja": lax.rem(c, nj)}
 
-        @pl.when(ka > 0)
+        @pl.loop(0, columns)
+        def _(c):
+            greet({**next_to(c), "ka": 0})
+
+        @pl.when(serves > 0)
         def _():
-            @pl.loop(0, columns)
+            @pl.loop(1, columns)
             def _(c):
-                greet({**next_to(c), "ka": 0})
-
-        @pl.loop(1, columns)
-        def _(c):
-            greet(next_to(c))
+                greet({**next_to(c), "ka": serves})
+
+            pl.when(other_root)(functools.partial(greet, {"ka": serves}))
 
     beside = [
         (ia > 0, {"ia": jnp.maximum(ia - 1, 0)}),
@@ -112,7 +116,7 @@
         (ja > 0, {"ja": jnp.maximum(ja - 1, 0)}),
         (ja < nj - 1, {"ja": jnp.minimum(ja + 1, nj - 1)}),
     ]
-    expected = jnp.where(is_root, 0, 1) + jnp.where(ka == 0, nk - 1, 0)
+    expected = jnp.where(own_root, 0, 1) + jnp.where(ka == 0, nk - 1, 0)
     for there, where in beside:
         pl.when(there)(functools.partial(greet, where))
         expected = expected + there.astype(jnp.int32)
@@ -169,31 +173,24 @@
             device_id=where, device_id_type=MESH,
         )
 
-    slots = [lax.rem(column - (i * nj + j) + columns, columns) for i, j in root_of]
+    slots = [lax.rem(column - i * nj + columns, columns) for i, _ in root_of]
     load_copies = [
-        to_root(l_own, l_all.at[slots[o]], 8 + o, many_sem.at[1], {"ia": root_of[o][0], "ja": root_of[o][1], "ka": o})
+        to_root(l_own, l_all.at[slots[o]], 8 + o, many_sem.at[1], {"ia": root_of[o][0], "ja": 0, "ka": root_of[o][1]})
         for o in range(nk)
     ]
-    slot = jnp.where(ka == 0, slots[0], slots[-1])
-    shape_copy = to_root(s_own, s_all.at[slot], 7, many_sem.at[0], {"ia": root_ia, "ja": root_ja})
+    slot = jnp.where(odd, slots[1], slots[0])
+    shape_copy = to_root(s_own, s_all.at[slot], 7, many_sem.at[0], {"ia": root_ia, "ja": 0, "ka": root_ka})
 
     @pl.when(ka == 0)
     def _():
-        for o, copy in enumerate(load_copies):
-            if o:
-                copy.start()
-            else:
-                pl.when(~is_root)(copy.start)
-
-    pl.when(~is_root)(shape_copy.start)
-
-    @pl.when(is_root)
+        for copy in load_copies:
+            copy.start()
+
+    pl.when(~own_root)(shape_copy.start)
+
+    @pl.when(own_root)
     def _():
         s_all[0] = s_own[...]
-
-        @pl.when(ka == 0)
-        def _():
-            l_all[0] = l_own[...]
 
     def halo(src, dst, index, where):
         return pltpu.make_async_remote_copy(
@@ -381,21 +378,18 @@
         pl.when(sends)(copy.wait_send)
     for copy in plane_copies:
         copy.wait_send()
-    pl.when(~is_root)(shape_copy.wait_send)
+    pl.when(~own_root)(shape_copy.wait_send)
 
     @pl.when(ka == 0)
     def _():
-        for o, copy in enumerate(load_copies):
-            if o:
-                copy.wait_send()
-            else:
-                pl.when(~is_root)(copy.wait_send)
+        for copy in load_copies:
+            copy.wait_send()
 
     near = min(4, nj)
     line = lax.rem(ia, lines)
-    order = [o % lines for o in (1, 4, 5, 2, 3, 6, 7, 0)][:lines] if lines == 8 else list(range(lines))
+    order = [o % lines for o in (7, 4, 6, 5, 1, 3, 2, 0)][:lines] if lines == 8 else list(range(lines))
     direct = [
-        {"ia": lax.rem(root_ia + o, lines), "ja": lax.rem(root_ja + j, near)}
+        {"ia": lax.rem(ia + o, lines), "ja": j, "ka": serves}
         for j in range(near)
         for o in order
         if j or o
@@ -408,10 +402,10 @@
     ]
     hands_on = (ia < lines) & (ja == near - 1)
 
-    def give(targets):
+    def give(source, targets):
         for where in targets:
             pltpu.make_async_remote_copy(
-                src_ref=g_own, dst_ref=g_own, send_sem=many_sem.at[4], recv_sem=many_sem.at[3],
+                src_ref=source, dst_ref=g_own, send_sem=many_sem.at[4], recv_sem=many_sem.at[3],
                 device_id=where, device_id_type=MESH,
             ).start()
 
@@ -422,40 +416,39 @@
 
     @pl.when(is_root)
     def _():
-        others = s_all.at[1:columns]
-        pltpu.make_async_copy(others, others, many_sem.at[0]).wait()
-
-        @pl.when(ka == 0)
+        @pl.when(own_root)
         def _():
-            loads = l_all.at[1:columns]
-            pltpu.make_async_copy(loads, loads, many_sem.at[1]).wait()
-
-        @pl.when(ka > 0)
+            others = s_all.at[1:columns]
+            pltpu.make_async_copy(others, others, many_sem.at[0]).wait()
+
+        @pl.when(other_root)
         def _():
-            pltpu.make_async_copy(l_all, l_all, many_sem.at[1]).wait()
-
+            pltpu.make_async_copy(s_all, s_all, many_sem.at[0]).wait()
+
+        pltpu.make_async_copy(l_all, l_all, many_sem.at[1]).wait()
         summed = jnp.sum(s_all[...] * l_all[...], axis=0)
         each = jnp.sum(summed, axis=1, keepdims=True)
         row = lax.broadcasted_iota(jnp.int32, (8, 128), 0)
-        g_own[...] = jnp.sum(jnp.where(lane == row, each, 0.0), axis=0, keepdims=True)
-
-        give(direct)
+        g_sum[...] = jnp.sum(jnp.where(lane == row, each, 0.0), axis=0, keepdims=True)
+        give(g_sum, direct)
+        beside_core = [{"ka": serves}]
+
+        @pl.when(other_root)
+        def _():
+            give(g_sum, beside_core)
+            sent(direct + beside_core)
+
+        @pl.when(own_root)
+        def _():
+            force[...] = g_sum[...]
+            sent(direct)
+
+    @pl.when(~own_root)
+    def _():
+        pltpu.make_async_copy(g_own, g_own, many_sem.at[3]).wait()
+        pl.when(hands_on)(functools.partial(give, g_own, passed))
         force[...] = g_own[...]
-        sent(direct)
-
-    @pl.when(~is_root)
-    def _():
-        pltpu.make_async_copy(g_own, g_own, many_sem.at[3]).wait()
-
-        @pl.when(hands_on)
-        def _():
-            give(passed)
-
-        force[...] = g_own[...]
-
-        @pl.when(hands_on)
-        def _():
-            sent(passed)
+        pl.when(hands_on)(functools.partial(sent, passed))
 
 
 def finish(scale, new, partial, out, force, sem):
@@ -501,6 +494,7 @@
                 pltpu.VMEM((ni * nj, 8, 128), f32),
                 pltpu.VMEM((ni * nj, 1, 128), f32),
                 row,
+                row,
                 pltpu.VMEM((5, lj, lk), f32),
                 pltpu.SemaphoreType.DMA((4,)),
                 pltpu.SemaphoreType.DMA((15 + nk,)),

time: 28 us -> 27.5 us (0.982)
  the two profiles are of different devices: /device:TPU:40 before, /device:TPU:6 now
where the time goes in v5:
time: 27.5 us; the launch traced here: 27.4 us
  Pallas kernels  26.8 us (97%)
  between operations  0.64 us (2%)
    pallas_call x1, Pallas kernels, local(): pl.pallas_call(functools.partial(section, sizes), out_shape=(pltpu.VMEM(f...  25.5 us
    pallas_call x1, Pallas kernels, local(): pl.pallas_call(functools.partial(finish, 1.0 / math.sqrt(ni * li * nj * l...  1.24 us

profile of v5, /device:TPU:6, one launch (start us, length us, event | category | flops | bytes accessed | tf_op | source)
XLA Modules:
  0.0 27.4 jit_solution(8483496658717583464)
XLA Ops:
  0.6 25.5 %section.1 = (f32[8,5,16,128]{3,2,1,0:T(8,128)S(1)}, f32[1,128]{1,0:T(1,128)S(1)}) custom-call(f32[8,5,16,128]{3,2,1,0:T(8,128)} %flow.1, f32[8,8,16]{2,1,0:T(8,128)} %shapes.1, f32[2,64]{1,0:T(2,128)} %coords_in.1, s32[8,16]{1,0:T(8,128)} %mask.1), custom_call_target="tpu_custom_call" | custom-call | tf_op jit(solution)/shard_map/section/pallas_call | solution.py:474
  26.1 1.2 %finish.1 = (f32[8,5,16,128]{3,2,1,0:T(8,128)}, f32[1,8]{1,0:T(1,128)}) custom-call(f32[8,5,16,128]{3,2,1,0:T(8,128)S(1)} %get-tuple-element.6.new, f32[1,128]{1,0:T(1,128)S(1)} %get-tuple-element.7.partial), custom_call_target="tpu_custom_call" | custom-call | tf_op jit(solution)/shard_map/finish/pallas_call | solution.py:510

commit v6 on v5

--- a/solution.py
+++ b/solution.py
@@ -59,7 +59,7 @@
     sizes, flow, shapes, coords_in, mask, new, force,
     fv, sv, mv, coords, prim, raw_i, raw_j, send_k, halo_k, edge_k, planes, planes_in,
     s_own, l_own, s_all, l_all, g_sum, g_own, flux_i,
-    local_sem, send_sem, recv_sem, many_sem, column_sem,
+    local_sem, send_sem, recv_sem, many_sem, column_sem, edge_sem,
 ):
     ni, nj, nk = sizes
     ia, ja, ka = lax.axis_index("ia"), lax.axis_index("ja"), lax.axis_index("ka")
@@ -117,9 +117,9 @@
         (ja < nj - 1, {"ja": jnp.minimum(ja + 1, nj - 1)}),
     ]
     expected = jnp.where(own_root, 0, 1) + jnp.where(ka == 0, nk - 1, 0)
-    for there, where in beside:
-        pl.when(there)(functools.partial(greet, where))
-        expected = expected + there.astype(jnp.int32)
+    for (below, _), (above, where) in (beside[0:2], beside[2:4]):
+        pl.when(above)(functools.partial(greet, where))
+        expected = expected + below.astype(jnp.int32)
     lead = nk // 2
     leads = ka == lead
     pl.when(~leads)(functools.partial(greet, {"ka": lead}))
@@ -158,7 +158,12 @@
         own_row = lane // lj == lax.broadcasted_iota(jnp.int32, (8, 128), 0)
         l_own[...] = jnp.sum(jnp.where(own_row & (keep == 1), flat, 0.0), axis=0, keepdims=True)
 
-    pl.semaphore_wait(barrier, expected)
+    pl.when(expected > 0)(functools.partial(pl.semaphore_wait, barrier, expected))
+    for axis, (there, where) in enumerate((beside[0], beside[2])):
+
+        @pl.when(there)
+        def _(axis=axis, where=where):
+            pl.semaphore_signal(edge_sem.at[axis], inc=1, device_id=where, device_id_type=MESH)
 
     @pl.when(leads)
     def _():
@@ -208,7 +213,7 @@
         (halo(send_k.at[0], halo_k.at[0], 4, {"ka": jnp.minimum(ka + 1, nk - 1)}), has_k1, has_k0),
         (halo(send_k.at[1], halo_k.at[1], 5, {"ka": jnp.maximum(ka - 1, 0)}), has_k0, has_k1),
     ]
-    for copy, sends, _ in copies[0:4]:
+    for copy, sends, _ in (copies[1], copies[3]):
         pl.when(sends)(copy.start)
 
     plane_copies = [
@@ -263,6 +268,12 @@
         copy.start()
     for copy, sends, _ in copies[4:6]:
         pl.when(sends)(copy.start)
+    for axis, (copy, sends, _) in ((1, copies[2]), (0, copies[0])):
+
+        @pl.when(sends)
+        def _(axis=axis, copy=copy):
+            pl.semaphore_wait(edge_sem.at[axis], 1)
+            copy.start()
 
     pltpu.make_async_copy(planes_in, planes_in, many_sem.at[2]).wait()
     total = planes[...]
@@ -501,6 +512,7 @@
                 pltpu.SemaphoreType.DMA((6,)),
                 pltpu.SemaphoreType.DMA((5,)),
                 pltpu.SemaphoreType.REGULAR,
+                pltpu.SemaphoreType.REGULAR((2,)),
             ],
             compiler_params=pltpu.CompilerParams(
                 collective_id=0, has_side_effects=True, vmem_limit_bytes=32 * 1024 * 1024

time: 27.5 us -> 26.8 us (0.975)
  Pallas kernels: 26.8 us -> 26 us
    pallas_call x1, Pallas kernels: 25.5 us -> 24.8 us  [local(): pl.pallas_call(functools.partial(section, sizes), out_shape=(pltpu.VMEM(f...]
where the time goes in v6:
time: 26.8 us; the launch traced here: 26.6 us
  Pallas kernels  26 us (97%)
  between operations  0.64 us (2%)
    pallas_call x1, Pallas kernels, local(): pl.pallas_call(functools.partial(section, sizes), out_shape=(pltpu.VMEM(f...  24.8 us
    pallas_call x1, Pallas kernels, local(): pl.pallas_call(functools.partial(finish, 1.0 / math.sqrt(ni * li * nj * l...  1.24 us

profile of v6, /device:TPU:6, one launch (start us, length us, event | category | flops | bytes accessed | tf_op | source)
XLA Modules:
  0.0 26.6 jit_solution(17801008662369721075)
XLA Ops:
  0.6 24.8 %section.1 = (f32[8,5,16,128]{3,2,1,0:T(8,128)S(1)}, f32[1,128]{1,0:T(1,128)S(1)}) custom-call(f32[8,5,16,128]{3,2,1,0:T(8,128)} %flow.1, f32[8,8,16]{2,1,0:T(8,128)} %shapes.1, f32[2,64]{1,0:T(2,128)} %coords_in.1, s32[8,16]{1,0:T(8,128)} %mask.1), custom_call_target="tpu_custom_call" | custom-call | tf_op jit(solution)/shard_map/section/pallas_call | solution.py:485
  25.4 1.2 %finish.1 = (f32[8,5,16,128]{3,2,1,0:T(8,128)}, f32[1,8]{1,0:T(1,128)}) custom-call(f32[8,5,16,128]{3,2,1,0:T(8,128)S(1)} %get-tuple-element.6.new, f32[1,128]{1,0:T(1,128)S(1)} %get-tuple-element.7.partial), custom_call_target="tpu_custom_call" | custom-call | tf_op jit(solution)/shard_map/finish/pallas_call | solution.py:522

commit v7 on v6

--- a/solution.py
+++ b/solution.py
@@ -144,6 +144,36 @@
     s_own[...] = packed
     planes[...] = jnp.concatenate([disp, speed, jnp.zeros((li, 128 - 2 * lj), jnp.float32)], axis=1)
 
+    pl.when(expected > 0)(functools.partial(pl.semaphore_wait, barrier, expected))
+    for axis, (there, where) in enumerate((beside[0], beside[2])):
+
+        @pl.when(there)
+        def _(axis=axis, where=where):
+            pl.semaphore_signal(edge_sem.at[axis], inc=1, device_id=where, device_id_type=MESH)
+
+    @pl.when(leads)
+    def _():
+        for o in range(1, nk):
+            pl.semaphore_signal(
+                column_sem, inc=1, device_id={"ka": lax.rem(ka + o, nk)}, device_id_type=MESH
+            )
+
+    def to_root(src, dst, sem_index, recv, where):
+        return pltpu.make_async_remote_copy(
+            src_ref=src, dst_ref=dst, send_sem=send_sem.at[sem_index], recv_sem=recv,
+            device_id=where, device_id_type=MESH,
+        )
+
+    slots = [lax.rem(column - i * nj + columns, columns) for i, _ in root_of]
+    load_copies = [
+        to_root(l_own, l_all.at[slots[o]], 8 + o, many_sem.at[1], {"ia": root_of[o][0], "ja": 0, "ka": root_of[o][1]})
+        for o in range(nk)
+    ]
+    slot = jnp.where(odd, slots[1], slots[0])
+    shape_copy = to_root(s_own, s_all.at[slot], 7, many_sem.at[0], {"ia": root_ia, "ja": 0, "ka": root_ka})
+
+    pl.when(~own_root)(shape_copy.start)
+
     in_flow.wait()
 
     @pl.when(ka == 0)
@@ -158,40 +188,10 @@
         own_row = lane // lj == lax.broadcasted_iota(jnp.int32, (8, 128), 0)
         l_own[...] = jnp.sum(jnp.where(own_row & (keep == 1), flat, 0.0), axis=0, keepdims=True)
 
-    pl.when(expected > 0)(functools.partial(pl.semaphore_wait, barrier, expected))
-    for axis, (there, where) in enumerate((beside[0], beside[2])):
-
-        @pl.when(there)
-        def _(axis=axis, where=where):
-            pl.semaphore_signal(edge_sem.at[axis], inc=1, device_id=where, device_id_type=MESH)
-
-    @pl.when(leads)
-    def _():
-        for o in range(1, nk):
-            pl.semaphore_signal(
-                column_sem, inc=1, device_id={"ka": lax.rem(ka + o, nk)}, device_id_type=MESH
-            )
-
-    def to_root(src, dst, sem_index, recv, where):
-        return pltpu.make_async_remote_copy(
-            src_ref=src, dst_ref=dst, send_sem=send_sem.at[sem_index], recv_sem=recv,
-            device_id=where, device_id_type=MESH,
-        )
-
-    slots = [lax.rem(column - i * nj + columns, columns) for i, _ in root_of]
-    load_copies = [
-        to_root(l_own, l_all.at[slots[o]], 8 + o, many_sem.at[1], {"ia": root_of[o][0], "ja": 0, "ka": root_of[o][1]})
-        for o in range(nk)
-    ]
-    slot = jnp.where(odd, slots[1], slots[0])
-    shape_copy = to_root(s_own, s_all.at[slot], 7, many_sem.at[0], {"ia": root_ia, "ja": 0, "ka": root_ka})
-
     @pl.when(ka == 0)
     def _():
         for copy in load_copies:
             copy.start()
-
-    pl.when(~own_root)(shape_copy.start)
 
     @pl.when(own_root)
     def _():

time: 26.8 us -> 26.8 us (level)
  no operation moved by 1% of the time
where the time goes in v7:
time: 26.8 us; the launch traced here: 26.6 us
  Pallas kernels  26 us (97%)
  between operations  0.64 us (2%)
    pallas_call x1, Pallas kernels, local(): pl.pallas_call(functools.partial(section, sizes), out_shape=(pltpu.VMEM(f...  24.8 us
    pallas_call x1, Pallas kernels, local(): pl.pallas_call(functools.partial(finish, 1.0 / math.sqrt(ni * li * nj * l...  1.24 us

profile of v7, /device:TPU:6, one launch (start us, length us, event | category | flops | bytes accessed | tf_op | source)
XLA Modules:
  0.0 26.6 jit_solution(10910460195784019521)
XLA Ops:
  0.6 24.8 %section.1 = (f32[8,5,16,128]{3,2,1,0:T(8,128)S(1)}, f32[1,128]{1,0:T(1,128)S(1)}) custom-call(f32[8,5,16,128]{3,2,1,0:T(8,128)} %flow.1, f32[8,8,16]{2,1,0:T(8,128)} %shapes.1, f32[2,64]{1,0:T(2,128)} %coords_in.1, s32[8,16]{1,0:T(8,128)} %mask.1), custom_call_target="tpu_custom_call" | custom-call | tf_op jit(solution)/shard_map/section/pallas_call | solution.py:485
  25.4 1.2 %finish.1 = (f32[8,5,16,128]{3,2,1,0:T(8,128)}, f32[1,8]{1,0:T(1,128)}) custom-call(f32[8,5,16,128]{3,2,1,0:T(8,128)S(1)} %get-tuple-element.6.new, f32[1,128]{1,0:T(1,128)S(1)} %get-tuple-element.7.partial), custom_call_target="tpu_custom_call" | custom-call | tf_op jit(solution)/shard_map/finish/pallas_call | solution.py:522
